TPU v7x, 32 devices: a whole 2x2x4 slice. The times are simulated.
32 devices in a mesh: ep: 8 (over z, y), tp: 4 (over x, core).
Axes of the slice: x: 2, y: 2, z: 4, core: 2. Of those that a mesh axis runs over, the one named last changes fastest.
Arguments:
- tokens: bfloat16 [4096, 2048], P('ep'), may hold values from -6 to 6
- lengths: int32 [14], replicated, may hold values from 1 to 1024, as said below
- routes: int32 [4096, 4], P('ep'), may hold values from 0 to 11, all different within a row; in each aligned block of 512 rows (0 to 511, 512 to 1023, ...) at most 240 rows name the same one
- attn_gain: bfloat16 [2048], P('ep'), may hold values from 0.25 to 1.75
- w_query: bfloat16 [2048, 2048], P('ep', 'tp'), may hold values from -0.125 to 0.125
- w_key: bfloat16 [2048, 2048], P('ep', 'tp'), may hold values from -0.125 to 0.125
- w_value: bfloat16 [2048, 2048], P('ep', 'tp'), may hold values from -0.125 to 0.125
- w_out: bfloat16 [2048, 2048], P('ep', 'tp'), may hold values from -1 to 1
- ffn_gain: bfloat16 [2048], P('ep'), may hold values from 0.25 to 1.75
- w_router: bfloat16 [2048, 12], P('ep'), may hold values from -0.0625 to 0.0625
- shared_mix: bfloat16 [2048], P('ep'), may hold values from -0.125 to 0.125
- shared_gate: bfloat16 [2048, 5632], P('ep', 'tp'), may hold values from -0.125 to 0.125
- shared_up: bfloat16 [2048, 5632], P('ep', 'tp'), may hold values from -0.125 to 0.125
- shared_down: bfloat16 [2048, 5632], P('ep', 'tp'), may hold values from -0.078125 to 0.078125
- expert_gate: bfloat16 [16, 1408, 2048], P('ep', 'tp'), may hold values from -0.125 to 0.125
- expert_up: bfloat16 [16, 1408, 2048], P('ep', 'tp'), may hold values from -0.125 to 0.125
- expert_down: bfloat16 [16, 1408, 2048], P('ep', 'tp'), may hold values from -3.5 to 3.5
- cotangent: bfloat16 [4096, 2048], P('ep'), may hold values from -6 to 6
Outputs:
- block_out: bfloat16 [4096, 2048], P('ep')
- grad_tokens: float32 [4096, 2048], P('ep')
- grad_attn_gain: float32 [2048], P('ep')
- grad_query: float32 [2048, 2048], P('ep', 'tp')
- grad_key: float32 [2048, 2048], P('ep', 'tp')
- grad_value: float32 [2048, 2048], P('ep', 'tp')
- grad_out: float32 [2048, 2048], P('ep', 'tp')
- grad_ffn_gain: float32 [2048], P('ep')
- grad_router: float32 [2048, 12], P('ep')
- grad_shared_mix: float32 [2048], P('ep')
- grad_shared_gate: float32 [2048, 5632], P('ep', 'tp')
- grad_shared_up: float32 [2048, 5632], P('ep', 'tp')
- grad_shared_down: float32 [2048, 5632], P('ep', 'tp')
- grad_expert_gate: float32 [16, 1408, 2048], P('ep', 'tp')
- grad_expert_up: float32 [16, 1408, 2048], P('ep', 'tp')
- grad_expert_down: float32 [16, 1408, 2048], P('ep', 'tp')
Inputs may be any that keep to these rules, and one draw needn't show every extreme that they name: `lengths`: the sequences lie end to end over all 4096 positions. One begins at position 0 and none at any other multiple of 512; every aligned block of 512 positions holds exactly two sequence starts except one block, neither the first nor the last, which holds none; exactly one sequence has 1024 tokens. `routes`: in each aligned block of 512 rows no expert is named by more than 240 rows, a bound that some block reaches.
All inputs are finite; a program needn't handle non-finite values.
Results may differ from a plain program's by a relative error of at most 0.018.
Values may be sent and summed in bfloat16 or wider, within the bound.
A program may use at most 384 MiB of HBM per device.

v0:
```python
import functools

import jax
import jax.numpy as jnp
from jax import lax
from jax.experimental import pallas as pl
from jax.experimental.pallas import tpu as pltpu
from jax.sharding import PartitionSpec as P

HD = 128


epsilon = 1e-06
rope_base = 1000000.0
highest = lax.Precision.HIGHEST
MESH = pl.DeviceIdType.MESH


def passed_along(block, axis, distance):
    devices = range(lax.axis_size(axis))
    route = [(i - distance, i) for i in devices if i - distance in devices]
    return lax.ppermute(block, axis, route)


def rope_tables(positions, width):
    steps = jnp.arange(0, width, 2, dtype=jnp.float32) / width
    inverse = rope_base ** (-steps)
    angles = positions.astype(jnp.float32)[:, None] * inverse[None, :]
    angles = jnp.concatenate([angles, angles], axis=-1)
    return (jnp.cos(angles)[:, None, :], jnp.sin(angles)[:, None, :])


def turn_half(values):
    middle = values.shape[-1] // 2
    return jnp.concatenate([-values[..., middle:], values[..., :middle]], axis=-1)


def rotate(values, cosine, sine):
    return values * cosine + turn_half(values) * sine


def unrotate(grads, cosine, sine):
    return grads * cosine - turn_half(grads * sine)


def sequence_info(lengths, indices):
    starts = jnp.cumsum(lengths) - lengths
    inside = starts[None, :] <= indices[:, None]
    segment = jnp.sum(inside.astype(jnp.int32), axis=1) - 1
    first = jnp.max(jnp.where(inside, starts[None, :], -1), axis=1)
    return (segment, indices - first)


def norm_forward(values, gain):
    scale = lax.rsqrt(jnp.mean(values * values, axis=-1, keepdims=True) + epsilon)
    return (values * scale * gain, scale)


def norm_backward(values, scale, gain, grads):
    unit = values * scale
    scaled = grads * gain
    inner = jnp.mean(scaled * unit, axis=-1, keepdims=True)
    return (scale * (scaled - unit * inner), jnp.sum(grads * unit, axis=0))


def deliver(rows):
    arrived_rows = lax.all_to_all(rows, "ep", split_axis=0, concat_axis=0, tiled=True)
    return arrived_rows


def bring_back(parts, target, rows_here, top_count):
    moved = lax.all_to_all(parts, "ep", split_axis=0, concat_axis=0, tiled=True)
    piece = moved.shape[3]
    return moved.reshape(-1, piece)[target].reshape(rows_here, top_count, piece)


def body(
    tokens,
    lengths,
    routes,
    attn_gain,
    w_query,
    w_key,
    w_value,
    w_out,
    ffn_gain,
    w_router,
    shared_mix,
    shared_gate,
    shared_up,
    shared_down,
    expert_gate,
    expert_up,
    expert_down,
    cotangent,
):
    rows_here = tokens.shape[0]
    width = tokens.shape[1]
    ep_count = lax.axis_size("ep")
    offset = lax.axis_index("ep") * rows_here
    slot_here = expert_gate.shape[0]
    top_count = routes.shape[1]
    gathered = (
        lax.all_gather(attn_gain, "ep", axis=0, tiled=True),
        lax.all_gather(w_query, "ep", axis=0, tiled=True),
        lax.all_gather(w_key, "ep", axis=0, tiled=True),
        lax.all_gather(w_value, "ep", axis=0, tiled=True),
        lax.all_gather(w_out, "ep", axis=0, tiled=True),
        lax.all_gather(ffn_gain, "ep", axis=0, tiled=True),
        lax.all_gather(w_router, "ep", axis=0, tiled=True),
        lax.all_gather(shared_mix, "ep", axis=0, tiled=True),
        lax.all_gather(shared_gate, "ep", axis=0, tiled=True),
        lax.all_gather(shared_up, "ep", axis=0, tiled=True),
        lax.all_gather(shared_down, "ep", axis=0, tiled=True),
    )
    (
        gain_first,
        query_weight_matrix,
        key_weight_matrix,
        value_weight_matrix,
        output_weight,
        gain_second,
        router_weight,
        shared_mixer_weight,
        shared_gate_weight,
        shared_up_weight,
        shared_down_weight,
    ) = gathered
    expert_count = router_weight.shape[1]
    capacity = (rows_here * top_count * 7 // (5 * expert_count) + 7) // 8 * 8
    heads_here = query_weight_matrix.shape[1] // HD
    score_scale = HD ** (-0.5)
    first_norm_scale = gain_first.astype(jnp.float32)
    second_norm_scale = gain_second.astype(jnp.float32)
    layer_input = tokens.astype(jnp.float32)
    normed_wide, norm_one = norm_forward(layer_input, first_norm_scale)
    normed_one = normed_wide.astype(jnp.bfloat16)
    query_at = offset + jnp.arange(rows_here, dtype=jnp.int32)
    key_at = offset - 2 * rows_here + jnp.arange(3 * rows_here, dtype=jnp.int32)
    query_seg, query_pos = sequence_info(lengths, query_at)
    key_seg, _ = sequence_info(lengths, key_at)
    cosine, sine = rope_tables(query_pos, HD)
    query_pre = jnp.dot(
        normed_one, query_weight_matrix, preferred_element_type=jnp.float32
    ).reshape(rows_here, heads_here, HD)
    key_pre = jnp.dot(normed_one, key_weight_matrix, preferred_element_type=jnp.float32).reshape(
        rows_here, heads_here, HD
    )
    queries = rotate(query_pre, cosine, sine).astype(jnp.bfloat16)
    keys = rotate(key_pre, cosine, sine).astype(jnp.bfloat16)
    values = (
        jnp.dot(normed_one, value_weight_matrix, preferred_element_type=jnp.float32)
        .astype(jnp.bfloat16)
        .reshape(rows_here, heads_here, HD)
    )
    carried = jnp.stack([keys, values], axis=0)
    window = [carried]
    for hop in range(2):
        carried = passed_along(carried, "ep", 1)
        window = [carried] + window
    joined = jnp.concatenate(window, axis=1)
    keys_win = joined[0]
    values_win = joined[1]
    allowed = (
        (query_seg[:, None] == key_seg[None, :])
        & (key_at[None, :] <= query_at[:, None])
        & (key_at[None, :] >= 0)
    )
    scores = (
        jnp.einsum("qhd,khd->hqk", queries, keys_win, preferred_element_type=jnp.float32)
        * score_scale
    )
    masked = jnp.where(allowed[None], scores, -1e30)
    peak = jnp.max(masked, axis=-1, keepdims=True)
    expo = jnp.exp(masked - peak)
    total = jnp.sum(expo, axis=-1, keepdims=True)
    log_total = peak + jnp.log(total)
    weights = expo / total
    attended = jnp.einsum(
        "hqk,khd->qhd", weights.astype(jnp.bfloat16), values_win, preferred_element_type=jnp.float32
    )
    attended = attended.reshape(rows_here, heads_here * HD).astype(jnp.bfloat16)
    attn_part = jnp.einsum("th,dh->td", attended, output_weight, preferred_element_type=jnp.float32)
    resid = layer_input + lax.psum(attn_part, "tp")
    normed_two_wide, norm_two = norm_forward(resid, second_norm_scale)
    normed_two = normed_two_wide.astype(jnp.bfloat16)
    normed_two_f = normed_two.astype(jnp.float32)
    router_f = router_weight.astype(jnp.float32)
    mix_f = shared_mixer_weight.astype(jnp.float32)
    router = jax.nn.softmax(jnp.dot(normed_two_f, router_f, precision=highest), axis=-1)
    picked = routes[:, :, None] == jnp.arange(expert_count, dtype=jnp.int32)[None, None, :]
    gates = jnp.sum(jnp.where(picked, router[:, None, :], 0.0), axis=-1)
    mixer = jax.nn.sigmoid(jnp.dot(normed_two_f, mix_f, precision=highest))
    shared_g = jnp.dot(normed_two, shared_gate_weight, preferred_element_type=jnp.float32)
    shared_u = jnp.dot(normed_two, shared_up_weight, preferred_element_type=jnp.float32)
    shared_h = (jax.nn.silu(shared_g) * shared_u).astype(jnp.bfloat16)
    shared_part = jnp.einsum(
        "tf,df->td", shared_h, shared_down_weight, preferred_element_type=jnp.float32
    )
    flat = routes.reshape(-1)
    hot = (flat[:, None] == jnp.arange(expert_count, dtype=jnp.int32)[None, :]).astype(jnp.int32)
    rank = jnp.sum(jnp.cumsum(hot, axis=0) * hot, axis=1) - 1
    target = flat * capacity + rank
    slot_total = ep_count * slot_here * capacity
    owner_route = (
        jnp.zeros((slot_total,), jnp.int32)
        .at[target]
        .set(jnp.arange(rows_here * top_count, dtype=jnp.int32))
    )
    filled = jnp.zeros((slot_total,), jnp.bool_).at[target].set(True)
    owner_token = owner_route // top_count
    send_rows = jnp.where(filled[:, None], normed_two[owner_token], jnp.zeros((), jnp.bfloat16))
    arrived_rows = deliver(send_rows.reshape(ep_count, slot_here, capacity, width))
    route_g = jnp.einsum(
        "nscd,sfd->nscf", arrived_rows, expert_gate, preferred_element_type=jnp.float32
    )
    route_u = jnp.einsum(
        "nscd,sfd->nscf", arrived_rows, expert_up, preferred_element_type=jnp.float32
    )
    route_h = (jax.nn.silu(route_g) * route_u).astype(jnp.bfloat16)
    route_part = jnp.einsum(
        "nscf,sfd->nscd", route_h, expert_down, preferred_element_type=jnp.float32
    )
    back_rows = bring_back(route_part, target, rows_here, top_count)
    upstream = cotangent.astype(jnp.float32)
    routed = jnp.sum(back_rows * gates[:, :, None], axis=1)
    ffn_part = mixer[:, None] * shared_part + routed
    route_dot = jnp.sum(back_rows * upstream[:, None, :], axis=-1)
    shared_dot = jnp.sum(shared_part * upstream, axis=-1)
    ffn_total, d_gate, d_mixer = lax.psum((ffn_part, route_dot, shared_dot), "tp")
    block_out = (resid + ffn_total).astype(jnp.bfloat16)
    d_router = jnp.sum(jnp.where(picked, d_gate[:, :, None], 0.0), axis=1)
    d_logits = router * (d_router - jnp.sum(router * d_router, axis=-1, keepdims=True))
    d_mixlogit = d_mixer * mixer * (1.0 - mixer)
    side = jnp.dot(d_logits, router_f.T, precision=highest) + d_mixlogit[:, None] * mix_f[None, :]
    grad_router = jnp.dot(normed_two_f.T, d_logits, precision=highest)
    grad_mix = jnp.dot(d_mixlogit, normed_two_f, precision=highest)
    d_shared = (mixer[:, None] * upstream).astype(jnp.bfloat16)
    d_sh = jnp.dot(d_shared, shared_down_weight, preferred_element_type=jnp.float32)
    sig_shared = jax.nn.sigmoid(shared_g)
    d_sg = (d_sh * shared_u * sig_shared * (1.0 + shared_g * (1.0 - sig_shared))).astype(
        jnp.bfloat16
    )
    d_su = (d_sh * shared_g * sig_shared).astype(jnp.bfloat16)
    d_normed_part = jnp.einsum(
        "tf,df->td", d_sg, shared_gate_weight, preferred_element_type=jnp.float32
    )
    d_normed_part = d_normed_part + jnp.einsum(
        "tf,df->td", d_su, shared_up_weight, preferred_element_type=jnp.float32
    )
    grad_sgate = jnp.einsum("td,tf->df", normed_two, d_sg, preferred_element_type=jnp.float32)
    grad_sup = jnp.einsum("td,tf->df", normed_two, d_su, preferred_element_type=jnp.float32)
    grad_sdown = jnp.einsum("td,tf->df", d_shared, shared_h, preferred_element_type=jnp.float32)
    d_route = (
        (gates[:, :, None] * upstream[:, None, :])
        .astype(jnp.bfloat16)
        .reshape(rows_here * top_count, width)
    )
    send_grads = jnp.where(filled[:, None], d_route[owner_route], jnp.zeros((), jnp.bfloat16))
    received_grads = deliver(send_grads.reshape(ep_count, slot_here, capacity, width))
    d_rh = jnp.einsum(
        "nscd,sfd->nscf", received_grads, expert_down, preferred_element_type=jnp.float32
    )
    sig_route = jax.nn.sigmoid(route_g)
    d_rg = (d_rh * route_u * sig_route * (1.0 + route_g * (1.0 - sig_route))).astype(jnp.bfloat16)
    routed_up_gradient = (d_rh * route_g * sig_route).astype(jnp.bfloat16)
    row_grads = jnp.einsum("nscf,sfd->nscd", d_rg, expert_gate, preferred_element_type=jnp.float32)
    row_grads = row_grads + jnp.einsum(
        "nscf,sfd->nscd", routed_up_gradient, expert_up, preferred_element_type=jnp.float32
    )
    grad_egate = jnp.einsum(
        "qxba,qxbr->xar", d_rg, arrived_rows, preferred_element_type=jnp.float32
    )
    expert_up_gradient = jnp.einsum(
        "qxba,qxbr->xar", routed_up_gradient, arrived_rows, preferred_element_type=jnp.float32
    )
    grad_edown = jnp.einsum(
        "qxba,qxbr->xar", route_h, received_grads, preferred_element_type=jnp.float32
    )
    grads_back = bring_back(row_grads, target, rows_here, top_count)
    d_routed = jnp.sum(grads_back, axis=1)
    d_normed_two = lax.psum(d_normed_part + d_routed, "tp") + side
    d_resid_norm, grad_gain_two = norm_backward(resid, norm_two, second_norm_scale, d_normed_two)
    d_resid = upstream + d_resid_norm
    d_resid_low = d_resid.astype(jnp.bfloat16)
    grad_outw = jnp.einsum("td,th->dh", d_resid_low, attended, preferred_element_type=jnp.float32)
    d_attended = jnp.einsum(
        "td,dh->th", d_resid_low, output_weight, preferred_element_type=jnp.float32
    )
    d_attended = d_attended.astype(jnp.bfloat16).reshape(rows_here, heads_here, HD)
    scores_again = (
        jnp.einsum("qhd,khd->hqk", queries, keys_win, preferred_element_type=jnp.float32)
        * score_scale
    )
    probs = jnp.where(allowed[None], jnp.exp(scores_again - log_total), 0.0)
    d_probs = jnp.einsum("qhd,khd->hqk", d_attended, values_win, preferred_element_type=jnp.float32)
    delta = jnp.sum(probs * d_probs, axis=-1, keepdims=True)
    d_scores = (probs * (d_probs - delta)).astype(jnp.bfloat16)
    d_queries = (
        jnp.einsum("hqk,khd->qhd", d_scores, keys_win, preferred_element_type=jnp.float32)
        * score_scale
    )
    d_keys_win = (
        jnp.einsum("hqk,qhd->khd", d_scores, queries, preferred_element_type=jnp.float32)
        * score_scale
    )
    d_values_win = jnp.einsum(
        "hqk,qhd->khd", probs.astype(jnp.bfloat16), d_attended, preferred_element_type=jnp.float32
    )
    pair_grads = jnp.stack([d_keys_win, d_values_win], axis=0)
    older = pair_grads[:, :rows_here]
    later = [pair_grads[:, rows_here : 2 * rows_here], pair_grads[:, 2 * rows_here :]]
    running = older
    for hop in range(2):
        running = passed_along(running, "ep", -1)
        running = running + later[hop]
    d_query_pre = (
        unrotate(d_queries, cosine, sine).astype(jnp.bfloat16).reshape(rows_here, heads_here * HD)
    )
    d_key_pre = (
        unrotate(running[0], cosine, sine).astype(jnp.bfloat16).reshape(rows_here, heads_here * HD)
    )
    d_values = running[1].astype(jnp.bfloat16).reshape(rows_here, heads_here * HD)
    grad_queryw = jnp.einsum(
        "td,th->dh", normed_one, d_query_pre, preferred_element_type=jnp.float32
    )
    grad_keyw = jnp.einsum("td,th->dh", normed_one, d_key_pre, preferred_element_type=jnp.float32)
    grad_valuew = jnp.einsum("td,th->dh", normed_one, d_values, preferred_element_type=jnp.float32)
    d_normed_one = jnp.einsum(
        "th,dh->td", d_query_pre, query_weight_matrix, preferred_element_type=jnp.float32
    )
    d_normed_one = d_normed_one + jnp.einsum(
        "th,dh->td", d_key_pre, key_weight_matrix, preferred_element_type=jnp.float32
    )
    d_normed_one = d_normed_one + jnp.einsum(
        "th,dh->td", d_values, value_weight_matrix, preferred_element_type=jnp.float32
    )
    d_normed_one = lax.psum(d_normed_one, "tp")
    d_input_norm, grad_gain_one = norm_backward(
        layer_input, norm_one, first_norm_scale, d_normed_one
    )
    grad_tokens = d_resid + d_input_norm
    summed = (
        lax.psum_scatter(grad_gain_one, "ep", scatter_dimension=0, tiled=True),
        lax.psum_scatter(grad_queryw, "ep", scatter_dimension=0, tiled=True),
        lax.psum_scatter(grad_keyw, "ep", scatter_dimension=0, tiled=True),
        lax.psum_scatter(grad_valuew, "ep", scatter_dimension=0, tiled=True),
        lax.psum_scatter(grad_outw, "ep", scatter_dimension=0, tiled=True),
        lax.psum_scatter(grad_gain_two, "ep", scatter_dimension=0, tiled=True),
        lax.psum_scatter(grad_router, "ep", scatter_dimension=0, tiled=True),
        lax.psum_scatter(grad_mix, "ep", scatter_dimension=0, tiled=True),
        lax.psum_scatter(grad_sgate, "ep", scatter_dimension=0, tiled=True),
        lax.psum_scatter(grad_sup, "ep", scatter_dimension=0, tiled=True),
        lax.psum_scatter(grad_sdown, "ep", scatter_dimension=0, tiled=True),
    )
    return (
        block_out,
        grad_tokens,
        summed[0],
        summed[1],
        summed[2],
        summed[3],
        summed[4],
        summed[5],
        summed[6],
        summed[7],
        summed[8],
        summed[9],
        summed[10],
        grad_egate,
        expert_up_gradient,
        grad_edown,
    )


class Place:
    def __init__(self):
        self.ep, self.tp = lax.axis_index("ep"), lax.axis_index("tp")
        self.z, self.y = self.ep // 2, self.ep % 2
        self.x, self.c = self.tp // 2, self.tp % 2
        self.depth = lax.axis_size("ep") // 2
        self.next_core = (self.ep, self.x * 2 + 1 - self.c)
        self.next_x = (self.ep, (1 - self.x) * 2 + self.c)
        self.next_y = (self.z * 2 + 1 - self.y, self.tp)

    def at_z(self, z):
        return (z * 2 + self.y, self.tp)

    def ahead(self, steps):
        return lax.rem(self.z + steps, self.depth)

    def behind(self, steps):
        return lax.rem(self.z + self.depth - steps, self.depth)

    def greet(self):
        barrier = pltpu.get_barrier_semaphore()
        peers = [self.next_core, self.next_x, self.next_y]
        peers += [self.at_z(self.ahead(k)) for k in range(1, self.depth)]
        for peer in peers:
            pl.semaphore_signal(barrier, inc=1, device_id=peer, device_id_type=MESH)
        pl.semaphore_wait(barrier, len(peers))

    def greet_row(self):
        barrier = pltpu.get_barrier_semaphore()
        count = 2 * self.depth
        peers = [(lax.rem(self.ep + k, count), self.tp) for k in range(1, count)]
        peers += [self.next_core, self.next_x]
        for peer in peers:
            pl.semaphore_signal(barrier, inc=1, device_id=peer, device_id_type=MESH)
        pl.semaphore_wait(barrier, len(peers))

    def greet_ep(self):
        barrier = pltpu.get_barrier_semaphore()
        count = 2 * self.depth
        for k in range(1, count):
            peer = (lax.rem(self.ep + k, count), self.tp)
            pl.semaphore_signal(barrier, inc=1, device_id=peer, device_id_type=MESH)
        pl.semaphore_wait(barrier, count - 1)


def remote(src, dst, send, recv, peer):
    return pltpu.make_async_remote_copy(
        src_ref=src, dst_ref=dst, send_sem=send, recv_sem=recv, device_id=peer, device_id_type=MESH
    )


def ffn_kernel(
    units,
    expert_count,
    rows_in,
    upstream_in,
    gate_in,
    up_in,
    down_in,
    pieces_in,
    weights_in,
    resid_in,
    gain_in,
    rows_all,
    weighted_out,
    d_pair_out,
    block_out,
    d_resid_low_out,
    d_resid_out,
    d_gain_out,
    d_side_out,
    d_rows_sum,
    out_sum,
    pair_w,
    down_w,
    side_w,
    rows_tile,
    upstream_tile,
    pair_pre,
    d_hidden,
    factors,
    dots,
    weighted_tile,
    d_pair_tile,
    d_resid_low,
    d_rows_tile,
    out_tile,
    d_rows_core,
    out_core,
    d_rows_held,
    out_held,
    d_rows_hop,
    out_hop,
    d_rows_hop2,
    out_hop2,
    d_rows_z,
    out_z,
    d_rows_to_z,
    out_to_z,
    gathered_send,
    gathered_recv,
    hop_send,
    hop_recv,
    weight_sem,
    end_sem,
    own_sem,
    z_send,
    z_recv,
    plane_send,
    plane_recv,
    load_sem,
    store_sem,
    sum_send,
    sum_recv,
    end_send,
    end_recv,
    core_credit,
    hop_credit,
    hop2_credit,
):
    at = Place()
    depth = at.depth
    quarter, width = rows_in.shape
    half = quarter // 2
    f32, bf16 = jnp.float32, jnp.bfloat16

    def weight_copies():
        hidden = down_w.shape[0]
        slot_here, slot_hidden, shared = units
        routed = slot_here * slot_hidden
        columns = pieces_in.shape[2]
        pairs = [(weights_in.at[:, pl.ds(weights_in.shape[1] - 128, 128)], side_w)]
        kinds = ((gate_in, pair_w, 0), (up_in, pair_w, hidden), (down_in, down_w, 0))
        for kind, (experts, into, first) in enumerate(kinds):
            pairs.append((experts, into.at[pl.ds(first, routed)]))
            here = pl.ds(first + routed, shared)
            for e in range(2 * depth):
                src = pieces_in.at[e, pl.ds(kind * shared, shared)]
                pairs.append((src, into.at[here, pl.ds(e * columns, columns)]))
        return [
            pltpu.make_async_copy(src, dst, weight_sem.at[i]) for i, (src, dst) in enumerate(pairs)
        ]

    def clear_rest():
        hidden = down_w.shape[0]
        used = units[0] * units[1] + units[2]
        for into, first in ((pair_w, 0), (pair_w, hidden), (down_w, 0)):
            if used < hidden:
                into[first + used : first + hidden] = jnp.zeros((hidden - used, width), bf16)

    for copy in weight_copies():
        copy.start()
    clear_rest()

    def block(j, y, x):
        return rows_all.at[at.behind(j), y, x, at.c]

    def plane_copy(j, kind):
        y, other_y = at.y, 1 - at.y
        own, other_x = at.x, 1 - at.x
        if kind == 0:
            src, peer = block(j, y, own), at.next_x
        elif kind == 1:
            src, peer = block(j, y, own), at.next_y
        elif kind == 2:
            src, peer = block(j, y, other_x).at[pl.ds(0, half)], at.next_y
        elif kind == 3:
            src, peer = block(j, other_y, own).at[pl.ds(half, half)], at.next_x
        else:
            src = block(j, other_y if kind >= 6 else y, other_x if kind % 2 else own)
            peer = at.next_core
        return remote(src, src, plane_send.at[j, kind], plane_recv.at[j, kind], peer)

    def z_copy(k):
        return remote(
            rows_in, block(0, at.y, at.x), z_send.at[k - 1], z_recv.at[k - 1], at.at_z(at.ahead(k))
        )

    def z_arrival(k):
        dst = block(k, at.y, at.x)
        return remote(dst, dst, z_send.at[k - 1], z_recv.at[k - 1], at.at_z(at.behind(k)))

    def begin(j):
        for kind in (0, 1, 4):
            plane_copy(j, kind).start()

    def spread(j):
        plane_copy(j, 0).wait_recv()
        plane_copy(j, 2).start()
        plane_copy(j, 5).start()
        plane_copy(j, 1).wait_recv()
        plane_copy(j, 3).start()
        plane_copy(j, 6).start()

    def begin_later(j):
        z_arrival(j).wait_recv()
        begin(j)

    def last_hop(j):
        plane_copy(j, 2).wait_recv()
        plane_copy(j, 3).wait_recv()
        plane_copy(j, 7).start()

    def near_ready(j):
        plane_copy(j, 4).wait_recv()
        plane_copy(j, 5).wait_recv()

    def far_ready(j):
        plane_copy(j, 6).wait_recv()
        plane_copy(j, 7).wait_recv()

    def parity(step):
        return lax.rem(step, 2)

    def slot_of(turn):
        return lax.rem(turn + 1, depth)

    def other_y(step):
        return lax.rem(parity(step) + (step // 2 + 1) // depth, 2)

    def tile_at(step):
        return at.behind(slot_of(step // 2)), lax.rem(at.y + other_y(step), 2)

    def load_rows(step):
        z, y = tile_at(step)
        return pltpu.make_async_copy(rows_all.at[z, y], rows_tile, load_sem.at[0])

    def load_upstream(step):
        z, y = tile_at(step)
        return pltpu.make_async_copy(upstream_in.at[z, y], upstream_tile, load_sem.at[1])

    def stores(step):
        z, y = tile_at(step)
        pairs = ((weighted_tile, weighted_out), (d_pair_tile, d_pair_out))
        return [
            pltpu.make_async_copy(src, dst.at[z, y], store_sem.at[i])
            for i, (src, dst) in enumerate(pairs)
        ]

    tiles, cores = (d_rows_tile, out_tile), (d_rows_core, out_core)
    helds, sums = (d_rows_held, out_held), (d_rows_sum, out_sum)
    hops, hops2, zs = (d_rows_hop, out_hop), (d_rows_hop2, out_hop2), (d_rows_z, out_z)
    to_zs = (d_rows_to_z, out_to_z)

    def sum_copy(a, kind, src, dst, peer):
        return remote(src, dst, sum_send.at[a, kind], sum_recv.at[a, kind], peer)

    def core_sum(a):
        return sum_copy(a, 0, tiles[a].at[:, 1 - at.c], cores[a], at.next_core)

    def row_hop(turn, other):
        y = lax.rem(at.y + other, 2)
        slot = parity(turn)
        src = d_rows_held.at[slot, y, 1 - at.x]
        return remote(
            src, d_rows_hop.at[slot, y], hop_send.at[slot, other], hop_recv.at[slot, other], at.next_x
        )

    def out_hop_sum(turn):
        slot = parity(turn)
        src = out_held.at[slot, 1 - at.y]
        return remote(
            src, out_hop.at[slot], hop_send.at[slot, 2], hop_recv.at[slot, 2], at.next_y
        )

    def hop2_sum(a, turn):
        slot = parity(turn)
        if a == 0:
            src, peer = helds[0].at[slot, 1 - at.y, at.x], at.next_y
        else:
            src, peer = helds[1].at[slot, at.y, 1 - at.x], at.next_x
        return sum_copy(a, 2, src, hops2[a], peer)

    def z_sum(a, turn):
        return remote(
            to_zs[a].at[parity(turn)],
            zs[a].at[turn],
            end_send.at[a, turn],
            end_recv.at[a, turn],
            at.at_z(at.behind(turn + 1)),
        )

    def allow(semaphore, peer):
        pl.semaphore_signal(semaphore, inc=1, device_id=peer, device_id_type=MESH)

    piece = 32

    def add(into, first, second):
        def body(i, carry):
            part = pl.ds(pl.multiple_of(i * piece, piece), piece)
            into[part] = first[part] + second[part]
            return carry

        lax.fori_loop(0, quarter // piece, body, 0)

    def after_core(step):
        turn = step // 2
        other = other_y(step)
        held, y = parity(turn), lax.rem(at.y + other, 2)

        @pl.when((parity(step) == 0) & (turn >= 2))
        def _():
            for a in (0, 1):
                pl.semaphore_wait(hop_credit.at[a], 1)

        for a in (0, 1):
            core_sum(a).wait()
            for x in (1 - at.x, at.x):
                add(helds[a].at[held, y, x], tiles[a].at[x, at.c], cores[a].at[x])
            if a == 0:
                row_hop(turn, other).start()
            else:

                @pl.when(other == 1)
                def _():
                    out_hop_sum(turn).start()

        @pl.when(step + 1 < 2 * depth)
        def _():
            allow(core_credit, at.next_core)

    def after_row_hop(turn, other):
        slot, y = parity(turn), lax.rem(at.y + other, 2)
        row_hop(turn, other).wait()
        into = d_rows_held.at[slot, y, at.x]
        add(into, into, d_rows_hop.at[slot, y])

    def after_out_hop(turn):
        slot = parity(turn)
        out_hop_sum(turn).wait()
        for x in (1 - at.x, at.x):
            into = out_held.at[slot, at.y, x]
            add(into, into, out_hop.at[slot, x])

    def may_hop2(turn, a):
        @pl.when(turn >= 1)
        def _():
            pl.semaphore_wait(hop2_credit.at[a], 1)

    def after_hop(turn):
        after_row_hop(turn, 1)
        may_hop2(turn, 0)
        hop2_sum(0, turn).start()
        after_row_hop(turn, 0)
        after_out_hop(turn)
        may_hop2(turn, 1)
        hop2_sum(1, turn).start()

        @pl.when(turn + 2 < depth)
        def _():
            allow(hop_credit.at[0], at.next_x)
            allow(hop_credit.at[1], at.next_y)

    def after_hop2(turn):
        slot = parity(turn)
        for a in (0, 1):
            hop2_sum(a, turn).wait()

            @pl.when(turn >= 2)
            def _():
                z_sum(a, turn - 2).wait_send()

            add(to_zs[a].at[slot], helds[a].at[slot, at.y, at.x], hops2[a])
            z_sum(a, turn).start()
        allow(hop2_credit.at[0], at.next_y)
        allow(hop2_credit.at[1], at.next_x)

    load_upstream(0).start()
    at.greet()
    z_copy(1).start()
    own_copy = pltpu.make_async_copy(rows_in, block(0, at.y, at.x), own_sem)
    own_copy.start()
    own_copy.wait()
    begin(0)
    begin_later(1)
    for k in range(2, depth):
        z_copy(k).start()
    spread(0)
    spread(1)
    near_ready(1)
    load_rows(0).start()
    for copy in weight_copies():
        copy.wait()

    tile_rows = 4 * quarter
    hidden_total = down_w.shape[0]
    lane = lax.broadcasted_iota(jnp.int32, (tile_rows, 128), 1)
    slot_here, slot_hidden, shared_hidden = units
    routed = slot_here * slot_hidden
    across = (((1,), (1,)), ((), ()))
    few = 16

    def gate_factors(rows, picked):
        logits = jnp.dot(rows, side_w[...], preferred_element_type=f32)
        chooses = (lane >= 3) & (lane < 3 + expert_count)
        peak = jnp.max(jnp.where(chooses, logits, -1e30), axis=1, keepdims=True)
        expo = jnp.where(chooses, jnp.exp(jnp.where(chooses, logits, peak) - peak), 0.0)
        routed_gate = expo / jnp.sum(expo, axis=1, keepdims=True) * picked.astype(f32)
        mix_pre = jnp.sum(jnp.where(lane == 2, logits, 0.0), axis=1, keepdims=True)
        result = jnp.where(lane == slot_here, 1.0 / (1.0 + jnp.exp(-mix_pre)), 0.0)
        for s in range(slot_here):
            chosen = lane == 3 + at.ep * slot_here + s
            gate = jnp.sum(jnp.where(chosen, routed_gate, 0.0), axis=1, keepdims=True)
            result = jnp.where(lane == s, gate, result)
        return result

    few_lane = lax.broadcasted_iota(jnp.int32, (few, 128), 1)
    bounds = [s * slot_hidden for s in range(slot_here)] + [routed, hidden_total]

    def owners(group):
        found = []
        for s in range(slot_here + 1):
            low, high = max(bounds[s] - group * 128, 0), min(bounds[s + 1] - group * 128, 128)
            if low < high:
                found.append((s, low, high))
        return found

    def hidden_rows(i, carry):
        here = pl.ds(pl.multiple_of(i * few, few), few)
        gates = [
            jnp.broadcast_to(factors[here, s : s + 1], (few, 128)) for s in range(slot_here + 1)
        ]
        parts = [None] * (slot_here + 1)
        for group in range(hidden_total // 128):
            units_here = slice(group * 128, (group + 1) * 128)
            units_up = slice(hidden_total + group * 128, hidden_total + (group + 1) * 128)
            gate_pre, up_pre = pair_pre[here, units_here], pair_pre[here, units_up]
            d_h = d_hidden[here, units_here]
            found = owners(group)
            factor = gates[found[0][0]]
            for s, low, _ in found[1:]:
                factor = jnp.where(few_lane >= low, gates[s], factor)
            sig = 0.5 + 0.5 * jnp.tanh(0.5 * gate_pre)
            silu = gate_pre * sig
            hidden = silu * up_pre
            product = hidden * d_h
            gated = factor * d_h
            weighted_tile[here, units_here] = (factor * hidden).astype(bf16)
            slope = sig + silu * (1.0 - sig)
            d_pair_tile[here, units_here] = (gated * up_pre * slope).astype(bf16)
            d_pair_tile[here, units_up] = (gated * silu).astype(bf16)
            for s, low, high in found:
                mine = product
                if high < 128:
                    mine = jnp.where(few_lane < high, mine, 0.0)
                if low > 0:
                    mine = jnp.where(few_lane >= low, mine, 0.0)
                parts[s] = mine if parts[s] is None else parts[s] + mine
        result = jnp.zeros((few, 128), f32)
        for s in range(slot_here + 1):
            dot = jnp.sum(parts[s], axis=1, keepdims=True)
            where = few_lane == (2 if s == slot_here else 3 + at.ep * slot_here + s)
            result = jnp.where(where, dot, result)
        dots[here] = result.astype(bf16)
        return carry

    def first_half(step):
        load_upstream(step).wait()
        upstream = upstream_tile[...].reshape(tile_rows, upstream_tile.shape[-1])
        d_hidden[...] = lax.dot_general(
            upstream[:, :width], down_w[...], across, preferred_element_type=f32
        )
        load_rows(step).wait()
        rows = rows_tile[...].reshape(tile_rows, width)
        factors[...] = gate_factors(rows, upstream[:, width:])
        pair_pre[...] = lax.dot_general(rows, pair_w[...], across, preferred_element_type=f32)

        @pl.when(step + 1 < 2 * depth)
        def _():
            load_upstream(step + 1).start()

        @pl.when(step >= 1)
        def _():
            for copy in stores(step - 1):
                copy.wait()

        lax.fori_loop(0, tile_rows // few, hidden_rows, 0, unroll=2)
        for copy in stores(step):
            copy.start()
        turn = step // 2

        @pl.when(step == 0)
        def _():
            last_hop(0)

        @pl.when((parity(step) == 0) & (turn + 1 < depth))
        def _():
            last_hop(turn + 1)

        @pl.when((step >= 1) & (step + 1 < depth))
        def _():
            spread(step + 1)

        @pl.when(step + 2 < depth)
        def _():
            begin_later(step + 2)

    def second_half(step):
        blocks = (2, 2, quarter)
        some = width // 2
        for n in range(2):
            columns = slice(n * some, (n + 1) * some)
            part = jnp.dot(weighted_tile[...], down_w[:, columns], preferred_element_type=f32)
            out_tile[:, :, :, columns] = part.astype(bf16).reshape(blocks + (some,))
            part = jnp.dot(d_pair_tile[...], pair_w[:, columns], preferred_element_type=f32)
            d_rows_tile[:, :, :, columns] = part.astype(bf16).reshape(blocks + (some,))
        d_rows_tile[:, :, :, width:] = dots[...].reshape(blocks + (128,))

        @pl.when(step >= 1)
        def _():
            pl.semaphore_wait(core_credit, 1)

        for a in (0, 1):
            core_sum(a).start()
        turn = step // 2

        @pl.when((parity(step) == 0) & (turn + 1 < depth))
        def _():
            far_ready(slot_of(turn))

        @pl.when((parity(step) == 1) & (turn + 1 < depth))
        def _():
            near_ready(slot_of(turn + 1))

        @pl.when(step == 2 * depth - 3)
        def _():
            far_ready(slot_of(turn + 1))

        @pl.when(step + 1 < 2 * depth)
        def _():
            load_rows(step + 1).start()

    def step_body(step, carry):
        first_half(step)

        @pl.when(step == 2 * depth - 1)
        def _():
            after_hop(depth - 2)

        @pl.when(step >= 1)
        def _():
            after_core(step - 1)

        second_half(step)
        odd = parity(step) == 1

        @pl.when(odd & (step >= 3) & (step < 2 * depth - 1))
        def _():
            after_hop((step - 3) // 2)

        @pl.when(jnp.logical_not(odd) & (step >= 4))
        def _():
            after_hop2((step - 4) // 2)

        return carry

    lax.fori_loop(0, 2 * depth, step_body, 0)
    last = depth - 1
    own_rows, own_upstream = rows_tile.at[0, 0], upstream_tile.at[0, 0]
    own_loads = [
        pltpu.make_async_copy(rows_in, own_rows, end_sem.at[0]),
        pltpu.make_async_copy(
            upstream_in.at[at.z, at.y, at.x, at.c], own_upstream, end_sem.at[1]
        ),
    ]
    for copy in own_loads:
        copy.start()
    after_hop2(last - 1)
    after_row_hop(last, 1)
    may_hop2(last, 0)
    hop2_sum(0, last).start()
    after_core(2 * depth - 1)
    after_out_hop(last)
    may_hop2(last, 1)
    hop2_sum(1, last).start()
    after_row_hop(last, 0)

    def total_of(a):
        hop2_sum(a, last).wait()
        held = helds[a].at[last % 2, at.y, at.x]
        for turn in range(last):
            z_sum(a, turn).wait_recv()

        def total_body(i, carry):
            part = pl.ds(pl.multiple_of(i * piece, piece), piece)
            total = held[part].astype(f32) + hops2[a][part].astype(f32)
            for k in range(last):
                total = total + zs[a][k, part].astype(f32)
            sums[a][part] = total
            return carry

        lax.fori_loop(0, quarter // piece, total_body, 0)

    total_of(0)
    own_lane = lax.broadcasted_iota(jnp.int32, (quarter, 128), 1)
    chooses = (own_lane >= 3) & (own_lane < 3 + expert_count)
    for copy in own_loads:
        copy.wait()
    rows = own_rows[...]
    logits = jnp.dot(rows, side_w[...], preferred_element_type=f32)
    peak = jnp.max(jnp.where(chooses, logits, -1e30), axis=1, keepdims=True)
    expo = jnp.where(chooses, jnp.exp(jnp.where(chooses, logits, peak) - peak), 0.0)
    router = expo / jnp.sum(expo, axis=1, keepdims=True)
    mixer = 1.0 / (1.0 + jnp.exp(-jnp.where(own_lane == 2, logits, 0.0)))
    gate_dots = d_rows_sum[:, width:]
    d_router = jnp.where(chooses, gate_dots * own_upstream[:, width:].astype(f32), 0.0)
    d_logits = router * (d_router - jnp.sum(router * d_router, axis=1, keepdims=True))
    d_mix = gate_dots * mixer * (1.0 - mixer)
    d_side = jnp.where(own_lane == 2, d_mix, jnp.where(chooses, d_logits, 0.0))
    d_side_out[...] = d_side
    high = d_side.astype(bf16)
    lower = (d_side - high.astype(f32)).astype(bf16)
    for split in (high, lower):
        d_rows_sum[:, :width] += lax.dot_general(
            split, side_w[...], across, preferred_element_type=f32
        )

    def end_body(i, carry):
        part = pl.ds(pl.multiple_of(i * few, few), few)
        resid = resid_in[part]
        scale = lax.rsqrt(jnp.mean(resid * resid, axis=1, keepdims=True) + epsilon)
        unit_rows = resid * scale
        grads = d_rows_sum[part, :width]
        scaled = grads * gain_in[...]
        inner = jnp.mean(scaled * unit_rows, axis=1, keepdims=True)
        d_resid = own_upstream[part, :width].astype(f32) + scale * (scaled - unit_rows * inner)
        d_resid_out[part] = d_resid
        d_resid_low[part] = d_resid.astype(bf16)
        return carry + jnp.sum(grads * unit_rows, axis=0, keepdims=True)

    d_gain_out[...] = lax.fori_loop(0, quarter // few, end_body, jnp.zeros((1, width), f32))

    def gather_copy(kind):
        if kind == 2:
            src = dst = d_resid_low_out.at[1 - at.x, at.c]
        else:
            src, dst = d_resid_low, d_resid_low_out.at[at.x, at.c]
        peer = at.next_x if kind == 0 else at.next_core
        return remote(src, dst, gathered_send.at[kind], gathered_recv.at[kind], peer)

    own_end = pltpu.make_async_copy(d_resid_low, d_resid_low_out.at[at.x, at.c], own_sem)
    own_end.start()
    for kind in (0, 1):
        gather_copy(kind).start()
    total_of(1)
    block_out[...] = (resid_in[...] + out_sum[...]).astype(bf16)
    gather_copy(0).wait_recv()
    gather_copy(2).start()
    own_end.wait()
    gather_copy(0).wait_send()
    gather_copy(1).wait()
    gather_copy(2).wait()
    for copy in stores(2 * depth - 1):
        copy.wait()
    for a in (0, 1):
        for turn in range(max(0, depth - 3), depth - 1):
            z_sum(a, turn).wait_send()
    for k in range(1, depth):
        z_copy(k).wait_send()

    def finish(j, carry):
        for kind in range(8):
            plane_copy(j, kind).wait_send()
        return carry

    lax.fori_loop(0, depth, finish, 0)


def ffn_over_all(rows, upstream_all, experts, pieces, weights, resid, gain, units, expert_count):
    quarter, width = rows.shape
    ep_count, tp_count = lax.axis_size("ep"), lax.axis_size("tp")
    depth = ep_count // 2
    hidden = -(-(units[0] * units[1] + units[2]) // 128) * 128
    bf16, f32 = jnp.bfloat16, jnp.float32
    wide = width + 128
    tile_rows = tp_count * quarter
    tokens = ep_count * tile_rows
    anywhere = pl.BlockSpec(memory_space=pl.ANY)
    in_vmem = pl.BlockSpec(memory_space=pltpu.VMEM)

    def both(*lead):
        return [pltpu.VMEM(lead + (quarter, columns), bf16) for columns in (wide, width)]

    dma = pltpu.SemaphoreType.DMA
    outs = pl.pallas_call(
        functools.partial(ffn_kernel, units, expert_count),
        out_shape=(
            jax.ShapeDtypeStruct((depth, 2, 2, 2, quarter, width), bf16),
            jax.ShapeDtypeStruct((depth, 2, tile_rows, hidden), bf16),
            jax.ShapeDtypeStruct((depth, 2, tile_rows, 2 * hidden), bf16),
            jax.ShapeDtypeStruct((quarter, width), bf16),
            jax.ShapeDtypeStruct((2, 2, quarter, width), bf16),
            jax.ShapeDtypeStruct((quarter, width), f32),
            jax.ShapeDtypeStruct((1, width), f32),
            jax.ShapeDtypeStruct((quarter, 128), f32),
        ),
        in_specs=[anywhere] * 7 + [in_vmem] * 2,
        out_specs=(anywhere,) * 3 + (in_vmem, anywhere) + (in_vmem,) * 3,
        scratch_shapes=[
            pltpu.VMEM((quarter, wide), f32),
            pltpu.VMEM((quarter, width), f32),
            pltpu.VMEM((2 * hidden, width), bf16),
            pltpu.VMEM((hidden, width), bf16),
            pltpu.VMEM((width, 128), bf16),
            pltpu.VMEM((2, 2, quarter, width), bf16),
            pltpu.VMEM((2, 2, quarter, wide), bf16),
            pltpu.VMEM((tile_rows, 2 * hidden), f32),
            pltpu.VMEM((tile_rows, hidden), f32),
            pltpu.VMEM((tile_rows, 128), f32),
            pltpu.VMEM((tile_rows, 128), bf16),
            pltpu.VMEM((tile_rows, hidden), bf16),
            pltpu.VMEM((tile_rows, 2 * hidden), bf16),
            pltpu.VMEM((quarter, width), bf16),
        ]
        + both(2, 2)
        + both(2)
        + both(2, 2, 2)
        + both(2, 2)
        + both()
        + both(depth - 1)
        + both(2)
        + [
            dma((3,)),
            dma((3,)),
            dma((2, 3)),
            dma((2, 3)),
            dma((4 + 6 * depth,)),
            dma((2,)),
            dma,
            dma((depth - 1,)),
            dma((depth - 1,)),
            dma((depth, 8)),
            dma((depth, 8)),
            dma((2,)),
            dma((2,)),
            dma((2, 3)),
            dma((2, 3)),
            dma((2, depth - 1)),
            dma((2, depth - 1)),
            pltpu.SemaphoreType.REGULAR,
            pltpu.SemaphoreType.REGULAR((2,)),
            pltpu.SemaphoreType.REGULAR((2,)),
        ],
        compiler_params=pltpu.CompilerParams(
            collective_id=1, has_side_effects=True, vmem_limit_bytes=62 * 2**20
        ),
        cost_estimate=pl.CostEstimate(
            flops=12 * tokens * width * hidden,
            bytes_accessed=10 * tokens * width,
            transcendentals=tokens * hidden,
        ),
        name="ffn_all_tokens",
    )(
        rows,
        upstream_all.reshape(depth, 2, 2, 2, quarter, wide),
        *[array.reshape(-1, width) for array in experts],
        pieces,
        weights,
        resid,
        gain,
    )
    rows_all, weighted, d_pair, block_out, d_resid_low, d_resid, d_gain, d_side = outs
    return (
        rows_all.reshape(tokens, width),
        weighted.reshape(tokens, hidden),
        d_pair.reshape(tokens, 2 * hidden),
        block_out,
        d_resid_low.reshape(tile_rows, width),
        d_resid,
        d_gain[0],
        d_side,
    )


def swap_copies(at, pieces_in, pieces_out, send_sem, recv_sem, leave):
    count = 2 * at.depth
    copies = []
    for k in range(1, count):
        to, back = lax.rem(at.ep + k, count), lax.rem(at.ep + count - k, count)
        if leave:
            src, dst, peer = pieces_in.at[to], pieces_out.at[at.ep], to
        else:
            src, dst, peer = pieces_in.at[back], pieces_out.at[back], back
        copies.append(remote(src, dst, send_sem.at[k], recv_sem.at[k], (peer, at.tp)))
    return copies


def weights_kernel(
    own_in,
    pieces_in,
    all_out,
    pieces_out,
    own_sem,
    z_send,
    z_recv,
    y_send,
    y_recv,
    swap_send,
    swap_recv,
):
    at = Place()
    depth = at.depth
    half = own_in.shape[0] // 2
    last = depth - 1

    def block(k, y, h):
        return all_out.at[at.z + k, y, pl.ds(h * half, half)]

    def z_copy(k, h, direction):
        if k == 0:
            src = own_in.at[pl.ds(h * half, half)]
        else:
            src = block(k, at.y, h)
        slot = last + k - direction
        return remote(
            src,
            block(k, at.y, h),
            z_send.at[last + k, h, (direction + 1) // 2],
            z_recv.at[slot, h],
            at.at_z(at.z + direction),
        )

    def z_arrival(k, h):
        direction = 1 if k > 0 else -1
        dst = block(k, at.y, h)
        return remote(
            dst, dst, z_send.at[last + k, h, 0], z_recv.at[last + k, h], at.at_z(at.z + direction)
        )

    def y_copy(k, h):
        src = own_in.at[pl.ds(h * half, half)] if k == 0 else block(k, at.y, h)
        return remote(
            src, block(k, at.y, h), y_send.at[last + k, h], y_recv.at[last + k, h], at.next_y
        )

    own_copies = [
        pltpu.make_async_copy(own_in, all_out.at[at.z, at.y], own_sem.at[0]),
        pltpu.make_async_copy(pieces_in.at[at.ep], pieces_out.at[at.ep], own_sem.at[1]),
    ]
    for copy in own_copies:
        copy.start()
    has_up, has_down = at.z + 1 < depth, at.z > 0
    at.greet_ep()

    for h in (0, 1):
        pl.when(has_up)(lambda: z_copy(0, h, 1).start())
        pl.when(has_down)(lambda: z_copy(0, h, -1).start())
        y_copy(0, h).start()
    swap = (at, pieces_in, pieces_out, swap_send, swap_recv)
    for copy in swap_copies(*swap, True):
        copy.start()
    for k in range(1, depth):
        for h in (0, 1):
            for sign in (-1, 1):
                there = at.z + sign * k
                exists = (there >= 0) & (there < depth)
                onward = at.z - sign
                goes_on = exists & (onward >= 0) & (onward < depth)

                @pl.when(exists)
                def _():
                    z_arrival(sign * k, h).wait_recv()

                @pl.when(goes_on)
                def _():
                    z_copy(sign * k, h, -sign).start()

                @pl.when(exists)
                def _():
                    y_copy(sign * k, h).start()

    for copy in own_copies:
        copy.wait()
    for copy in swap_copies(*swap, False):
        copy.wait_recv()
    for copy in swap_copies(*swap, True):
        copy.wait_send()
    for h in (0, 1):
        pl.when(has_up)(lambda: z_copy(0, h, 1).wait_send())
        pl.when(has_down)(lambda: z_copy(0, h, -1).wait_send())
    for k in range(-last, depth):
        there = at.z + k
        exists = (there >= 0) & (there < depth)
        sign = 1 if k > 0 else -1
        onward = at.z - sign
        goes_on = exists & (onward >= 0) & (onward < depth)
        for h in (0, 1):

            @pl.when(exists)
            def _():
                y_copy(k, h).wait()

            if k != 0:

                @pl.when(goes_on)
                def _():
                    z_copy(k, h, -sign).wait_send()


def gather_over_ep(block, pieces):
    rows, columns = block.shape
    depth = lax.axis_size("ep") // 2
    anywhere = pl.BlockSpec(memory_space=pl.ANY)
    slots = 2 * depth - 1
    out, pieces = pl.pallas_call(
        weights_kernel,
        out_shape=(
            jax.ShapeDtypeStruct((depth, 2, rows, columns), block.dtype),
            jax.ShapeDtypeStruct(pieces.shape, pieces.dtype),
        ),
        in_specs=[anywhere] * 2,
        out_specs=(anywhere,) * 2,
        scratch_shapes=[
            pltpu.SemaphoreType.DMA((2,)),
            pltpu.SemaphoreType.DMA((slots, 2, 2)),
            pltpu.SemaphoreType.DMA((slots, 2)),
            pltpu.SemaphoreType.DMA((slots, 2)),
            pltpu.SemaphoreType.DMA((slots, 2)),
            pltpu.SemaphoreType.DMA((2 * depth,)),
            pltpu.SemaphoreType.DMA((2 * depth,)),
        ],
        compiler_params=pltpu.CompilerParams(collective_id=3, has_side_effects=True),
        cost_estimate=pl.CostEstimate(
            flops=0, bytes_accessed=8 * depth * rows * columns, transcendentals=0
        ),
        name="gather_weights",
    )(block, pieces)
    return out.reshape(2 * depth * rows, columns), pieces


class RowGather:
    def __init__(self, at, mine, everywhere, z_send, z_recv, plane_send, plane_recv):
        self.at, self.mine, self.everywhere = at, mine, everywhere
        self.z_sems, self.plane_sems = (z_send, z_recv), (plane_send, plane_recv)
        self.half = mine.shape[0] // 2

    def block(self, j, y, x):
        return self.everywhere.at[self.at.behind(j), y, x, self.at.c]

    def plane_copy(self, j, kind):
        at, half = self.at, self.half
        if kind == 0:
            src, peer = self.block(j, at.y, at.x), at.next_x
        elif kind == 1:
            src, peer = self.block(j, at.y, at.x), at.next_y
        elif kind == 2:
            src, peer = self.block(j, at.y, 1 - at.x).at[pl.ds(0, half)], at.next_y
        elif kind == 3:
            src, peer = self.block(j, 1 - at.y, at.x).at[pl.ds(half, half)], at.next_x
        else:
            y, x = 1 - at.y if kind >= 6 else at.y, 1 - at.x if kind % 2 else at.x
            src, peer = self.block(j, y, x), at.next_core
        send, recv = self.plane_sems
        return remote(src, src, send.at[j, kind], recv.at[j, kind], peer)

    def z_copy(self, k):
        send, recv = self.z_sems
        dst = self.block(0, self.at.y, self.at.x)
        peer = self.at.at_z(self.at.ahead(k))
        return remote(self.mine, dst, send.at[k - 1], recv.at[k - 1], peer)

    def begin(self, j):
        if j > 0:
            send, recv = self.z_sems
            dst = self.block(j, self.at.y, self.at.x)
            peer = self.at.at_z(self.at.behind(j))
            remote(dst, dst, send.at[j - 1], recv.at[j - 1], peer).wait_recv()
        for kind in (0, 1, 4):
            self.plane_copy(j, kind).start()

    def spread(self, j):
        self.plane_copy(j, 0).wait_recv()
        self.plane_copy(j, 2).start()
        self.plane_copy(j, 5).start()
        self.plane_copy(j, 1).wait_recv()
        self.plane_copy(j, 3).start()
        self.plane_copy(j, 6).start()

    def last_hop(self, j):
        self.plane_copy(j, 2).wait_recv()
        self.plane_copy(j, 3).wait_recv()
        self.plane_copy(j, 7).start()

    def finish(self):
        for k in range(1, self.at.depth):
            self.z_copy(k).wait_send()
        for j in range(self.at.depth):
            for kind in range(8):
                if kind >= 4:
                    self.plane_copy(j, kind).wait_recv()
                self.plane_copy(j, kind).wait_send()


def front_kernel(
    score_scale,
    block_in,
    weights_in,
    upstream_in,
    cos_in,
    sin_in,
    query_start,
    query_at,
    tokens_in,
    first_gain,
    gain_in,
    upstream_all,
    turned_out,
    k_out,
    v_out,
    q_out,
    lse_out,
    attended_out,
    resid_out,
    rows_out,
    normed,
    turned,
    qkv_w,
    out_w,
    k_all,
    v_all,
    scores_of,
    part,
    core_got,
    x_got,
    load_sem,
    z_send,
    z_recv,
    plane_send,
    plane_recv,
    kv_send,
    kv_recv,
    tp_send,
    tp_recv,
):
    at = Place()
    depth = at.depth
    count = 2 * depth
    heads, tokens, head = q_out.shape
    heads_width = heads * head
    windows = k_all.shape[1] // tokens
    quarter, width = resid_out.shape
    f32, bf16 = jnp.float32, jnp.bfloat16
    across = (((1,), (1,)), ((), ()))
    gather = RowGather(at, upstream_in, upstream_all, z_send, z_recv, plane_send, plane_recv)
    own = (windows - 1) * tokens

    def kv_copy(kind, w):
        held = (k_all, v_all)[kind]
        return remote(
            held.at[:, pl.ds(own, tokens)],
            held.at[:, pl.ds(w * tokens, tokens)],
            kv_send.at[kind, w],
            kv_recv.at[kind, w],
            (at.ep + (windows - 1 - w), at.tp),
        )

    def kv_arrival(kind, w):
        dst = (k_all, v_all)[kind].at[:, pl.ds(w * tokens, tokens)]
        peer = (at.ep - (windows - 1 - w), at.tp)
        return remote(dst, dst, kv_send.at[kind, w], kv_recv.at[kind, w], peer)

    def core_copy():
        return remote(part.at[:, 1 - at.c], core_got, tp_send.at[0], tp_recv.at[0], at.next_core)

    def x_copy():
        return remote(part.at[1 - at.x, at.c], x_got, tp_send.at[1], tp_recv.at[1], at.next_x)

    pairs = (
        (block_in, normed),
        (weights_in.at[:, pl.ds(0, 3 * heads_width)], qkv_w),
        (weights_in.at[:, pl.ds(3 * heads_width, heads_width)], out_w),
    )
    loads = [pltpu.make_async_copy(src, dst, load_sem.at[i]) for i, (src, dst) in enumerate(pairs)]
    for copy in loads:
        copy.start()
    at.greet_row()
    own_copy = pltpu.make_async_copy(
        upstream_in, gather.block(0, at.y, at.x), load_sem.at[len(pairs)]
    )
    own_copy.start()
    gather.z_copy(1).start()
    own_copy.wait()
    gather.begin(0)
    loads[0].wait()
    few = 16

    def norm_body(i, carry):
        here = pl.ds(pl.multiple_of(i * few, few), few)
        inputs = normed[here].astype(f32)
        scale = lax.rsqrt(jnp.mean(inputs * inputs, axis=1, keepdims=True) + epsilon)
        normed[here] = (inputs * scale * first_gain[...]).astype(bf16)
        return carry

    lax.fori_loop(0, tokens // few, norm_body, 0, unroll=2)
    loads[1].wait()
    lane = lax.broadcasted_iota(jnp.int32, (tokens, head), 1)
    sign = jnp.where(lane < head // 2, -1.0, 1.0)

    def rotated(array):
        return array * cos_in[...] + pltpu.roll(array, head // 2, 1) * sign * sin_in[...]

    keys = jnp.dot(
        normed[...], qkv_w[:, heads_width : 2 * heads_width], preferred_element_type=f32
    )
    for h in range(heads):
        k_all[h, own:] = rotated(keys[:, h * head : (h + 1) * head]).astype(bf16)
    values = jnp.dot(normed[...], qkv_w[:, 2 * heads_width :], preferred_element_type=f32)
    for h in range(heads):
        v_all[h, own:] = values[:, h * head : (h + 1) * head].astype(bf16)
    for w in reversed(range(windows - 1)):

        @pl.when(at.ep + (windows - 1 - w) < count)
        def _():
            for kind in (0, 1):
                kv_copy(kind, w).start()

    for k in range(2, depth):
        gather.z_copy(k).start()
    gather.spread(0)
    queries = jnp.dot(normed[...], qkv_w[:, :heads_width], preferred_element_type=f32)
    for h in range(heads):
        q_out[h] = rotated(queries[:, h * head : (h + 1) * head]).astype(bf16)
    gather.last_hop(0)
    gather.begin(1)
    turned[...] = normed[...].T
    turned_copy = pltpu.make_async_copy(turned, turned_out, load_sem.at[0])
    turned_copy.start()
    gather.spread(1)
    for w in range(windows - 1):

        @pl.when(at.ep < windows - 1 - w)
        def _():
            for held in (k_all, v_all):
                held[:, w * tokens : (w + 1) * tokens] = jnp.zeros((heads, tokens, head), bf16)

        @pl.when(at.ep >= windows - 1 - w)
        def _():
            for kind in (0, 1):
                kv_arrival(kind, w).wait_recv()

    outs = [
        pltpu.make_async_copy(src, dst, load_sem.at[i])
        for i, (src, dst) in ((1, (k_all, k_out)), (3, (v_all, v_out)))
    ]
    for copy in outs:
        copy.start()
    due = [functools.partial(gather.last_hop, 1)]
    for j in range(2, depth):
        due.append(functools.partial(gather.begin, j))
        due.append(functools.partial(gather.spread, j))
        due.append(functools.partial(gather.last_hop, j))

    def head_body(h, carry):
        q = q_out[h]
        peak = jnp.full((1, tokens), -1e30, f32)
        for w in range(windows):
            some = slice(w * tokens, (w + 1) * tokens)
            scores = lax.dot_general(k_all[h, some], q, across, preferred_element_type=f32)
            key_at = lax.broadcasted_iota(jnp.int32, scores.shape, 0)
            key_at = key_at + (at.ep + w + 1 - windows) * tokens
            allowed = (key_at >= query_start[...]) & (key_at <= query_at[...])
            scores = jnp.where(allowed, scores * score_scale, -1e30)
            scores_of[w] = scores
            peak = jnp.maximum(peak, jnp.max(scores, axis=0, keepdims=True))
        total = jnp.zeros((1, tokens), f32)
        for w in range(windows):
            expo = jnp.exp(scores_of[w] - peak)
            scores_of[w] = expo
            total = total + jnp.sum(expo, axis=0, keepdims=True)
        lse_out[h] = peak + jnp.log(total)
        each = 1.0 / total
        attended = jnp.zeros((head, tokens), f32)
        for w in range(windows):
            some = slice(w * tokens, (w + 1) * tokens)
            probs = (scores_of[w] * each).astype(bf16)
            attended = attended + jnp.dot(
                v_all[h, some].T, probs, preferred_element_type=f32
            )
        here = pl.ds(pl.multiple_of(h * head, head), head)
        attended_out[:, here] = attended.T.astype(bf16)
        for i in range(heads):

            @pl.when(h == i)
            def _():
                for action in due[i : i + 1]:
                    action()

        return carry

    lax.fori_loop(0, heads, head_body, 0)
    loads[2].wait()
    strips = 4
    strip = width // strips
    for n in range(strips):
        some = slice(n * strip, (n + 1) * strip)
        product = lax.dot_general(
            attended_out[...], out_w[some], across, preferred_element_type=f32
        )
        part[:, :, :, some] = product.astype(bf16).reshape(2, 2, quarter, strip)
    core_copy().start()
    rest = due[heads:]
    for action in rest[:2]:
        action()
    core_copy().wait()
    for x in (0, 1):
        part[x, at.c] = part[x, at.c] + core_got[x]
    x_copy().start()
    for action in rest[2:]:
        action()
    x_copy().wait()

    def end_body(i, carry):
        here = pl.ds(pl.multiple_of(i * few, few), few)
        total = part[at.x, at.c, here].astype(f32) + x_got[here].astype(f32)
        resid = tokens_in[here].astype(f32) + total
        scale = lax.rsqrt(jnp.mean(resid * resid, axis=1, keepdims=True) + epsilon)
        resid_out[here] = resid
        rows_out[here] = (resid * scale * gain_in[...]).astype(bf16)
        return carry

    lax.fori_loop(0, quarter // few, end_body, 0)
    turned_copy.wait()
    for copy in outs:
        copy.wait()
    for w in range(windows - 1):

        @pl.when(at.ep + (windows - 1 - w) < count)
        def _():
            for kind in (0, 1):
                kv_copy(kind, w).wait_send()

    gather.finish()


def attention_front(block, weights, upstream, in_place, heads, scale):
    tokens, width = block.shape
    quarter, wide = upstream.shape
    depth = lax.axis_size("ep") // 2
    head, windows = HD, 3
    f32, bf16 = jnp.float32, jnp.bfloat16
    anywhere = pl.BlockSpec(memory_space=pl.ANY)
    in_vmem = pl.BlockSpec(memory_space=pltpu.VMEM)
    dma = pltpu.SemaphoreType.DMA
    shape = jax.ShapeDtypeStruct
    window = (heads, windows * tokens, head)
    outs = pl.pallas_call(
        functools.partial(front_kernel, scale),
        out_shape=(
            shape((depth, 2, 2, 2, quarter, wide), bf16),
            shape((width, tokens), bf16),
            shape(window, bf16),
            shape(window, bf16),
            shape((heads, tokens, head), bf16),
            shape((heads, 1, tokens), f32),
            shape((tokens, heads * head), bf16),
            shape((quarter, width), f32),
            shape((quarter, width), bf16),
        ),
        in_specs=[anywhere] * 3 + [in_vmem] * len(in_place),
        out_specs=(anywhere,) * 4 + (in_vmem,) * 5,
        scratch_shapes=[
            pltpu.VMEM((tokens, width), bf16),
            pltpu.VMEM((width, tokens), bf16),
            pltpu.VMEM((width, 3 * heads * head), bf16),
            pltpu.VMEM((width, heads * head), bf16),
            pltpu.VMEM(window, bf16),
            pltpu.VMEM(window, bf16),
            pltpu.VMEM((windows, tokens, tokens), f32),
            pltpu.VMEM((2, 2, quarter, width), bf16),
            pltpu.VMEM((2, quarter, width), bf16),
            pltpu.VMEM((quarter, width), bf16),
            dma((4,)),
            dma((depth - 1,)),
            dma((depth - 1,)),
            dma((depth, 8)),
            dma((depth, 8)),
            dma((2, windows - 1)),
            dma((2, windows - 1)),
            dma((2,)),
            dma((2,)),
        ],
        compiler_params=pltpu.CompilerParams(
            collective_id=5, has_side_effects=True, vmem_limit_bytes=50 * 2**20
        ),
        cost_estimate=pl.CostEstimate(
            flops=8 * tokens * width * heads * head,
            bytes_accessed=2 * 8 * depth * quarter * wide,
            transcendentals=heads * tokens * windows * tokens,
        ),
        name="attention_front",
    )(block, weights, upstream, *in_place)
    return (outs[0].reshape(8 * depth * quarter, wide),) + tuple(outs[1:])


def back_kernel(
    units,
    score_scale,
    d_low_in,
    weights_in,
    q_in,
    k_in,
    v_in,
    turned_in,
    block_in,
    rows_in,
    d_pair_in,
    upstream_in,
    weighted_in,
    lse_in,
    query_start,
    query_at,
    cos_in,
    sin_in,
    own_rows_in,
    gain_in,
    d_resid_in,
    gain_two_in,
    side_in,
    out,
    small_out,
    block_out,
    d_rows_out,
    pieces_got,
    gate_out,
    up_out,
    down_out,
    qkv_w,
    turned,
    d_out,
    d_got,
    d_own,
    d_proj,
    part,
    core_got,
    x_got,
    d_rows,
    own,
    y_out,
    hop,
    from_z,
    small_own,
    small_hop,
    small_z,
    small,
    small_got,
    pieces,
    load_sem,
    d_send,
    d_recv,
    tp_send,
    tp_recv,
    y_send,
    y_recv,
    z_send,
    z_recv,
    little_send,
    little_recv,
    small_send,
    small_recv,
    swap_send,
    swap_recv,
    rows_send,
    rows_recv,
    own_sem,
    tile_sem,
    store_sem,
    strip_sem,
):
    at = Place()
    depth = at.depth
    count = 2 * depth
    heads, tokens, head = q_in.shape
    heads_width = heads * head
    windows = k_in.shape[1] // tokens
    quarter, width = d_rows.shape
    rows = out.shape[0]
    f32, bf16 = jnp.float32, jnp.bfloat16
    across = (((1,), (1,)), ((), ()))
    slot_here, slot_hidden, shared_hidden = units
    routed = slot_here * slot_hidden
    hidden = weighted_in.shape[2]
    few = 16

    def d_copy(w, h):
        peer = (at.ep - (2 - w), at.tp)
        return remote(d_out.at[w, h], d_got.at[w, h], d_send.at[w, h], d_recv.at[w, h], peer)

    def d_arrival(w, h):
        peer = (at.ep + (2 - w), at.tp)
        dst = d_got.at[w, h]
        return remote(dst, dst, d_send.at[w, h], d_recv.at[w, h], peer)

    def core_copy():
        return remote(part.at[:, 1 - at.c], core_got, tp_send.at[0], tp_recv.at[0], at.next_core)

    def x_copy():
        return remote(part.at[1 - at.x, at.c], x_got, tp_send.at[1], tp_recv.at[1], at.next_x)

    cuts = (pl.ds(0, heads_width), pl.ds(heads_width, 2 * heads_width))

    def y_copy(q, j):
        return remote(
            y_out.at[j, :, cuts[q]], hop.at[j, :, cuts[q]], y_send.at[q, j], y_recv.at[q, j], at.next_y
        )

    def z_copy(q, j):
        return remote(
            own.at[j, :, cuts[q]],
            from_z.at[j - 1, :, cuts[q]],
            z_send.at[q, j],
            z_recv.at[q, j],
            at.at_z(at.ahead(j)),
        )

    def little_y(j):
        return remote(
            small_own.at[at.ahead(j), 1 - at.y],
            small_hop.at[j],
            little_send.at[0, j],
            little_recv.at[0, j],
            at.next_y,
        )

    def little_z(j):
        return remote(
            small_own.at[at.ahead(j), at.y],
            small_z.at[j - 1],
            little_send.at[1, j],
            little_recv.at[1, j],
            at.at_z(at.ahead(j)),
        )

    def small_copy(kind):
        peer = at.next_core if kind == 0 else at.next_x
        return remote(
            small.at[kind], small_got.at[kind], small_send.at[kind], small_recv.at[kind], peer
        )

    ends = ((block_in, block_out), (d_rows, d_rows_out))

    def rows_copy(a, kind):
        mine, gathered = ends[a]
        if kind == 2:
            src = dst = gathered.at[1 - at.x, at.c]
        else:
            src, dst = mine, gathered.at[at.x, at.c]
        peer = at.next_x if kind == 0 else at.next_core
        return remote(src, dst, rows_send.at[a, kind], rows_recv.at[a, kind], peer)

    def rows_own(a):
        mine, gathered = ends[a]
        return pltpu.make_async_copy(mine, gathered.at[at.x, at.c], own_sem.at[a])

    def rows_begin(a):
        for kind in (0, 1):
            rows_copy(a, kind).start()
        rows_own(a).start()

    def rows_pass_on(a):
        rows_copy(a, 0).wait_recv()
        rows_copy(a, 2).start()

    def rows_end(a):
        rows_own(a).wait()
        rows_copy(a, 0).wait_send()
        rows_copy(a, 1).wait()
        rows_copy(a, 2).wait()

    def swap_copies(p, leave):
        some = pl.ds(p * shared_hidden, shared_hidden)
        copies = []
        for k in range(1, count):
            to, back = lax.rem(at.ep + k, count), lax.rem(at.ep + count - k, count)
            if leave:
                src, dst, peer = pieces.at[to, some], pieces_got.at[at.ep, some], to
            else:
                src, dst, peer = pieces.at[back, some], pieces_got.at[back, some], back
            copies.append(remote(src, dst, swap_send.at[p, k], swap_recv.at[p, k], (peer, at.tp)))
        return copies

    def swap_own(p):
        some = pl.ds(p * shared_hidden, shared_hidden)
        return pltpu.make_async_copy(
            pieces.at[at.ep, some], pieces_got.at[at.ep, some], own_sem.at[2 + p]
        )

    strips = 4
    strip = width // strips

    def load_strip(n):
        src = weights_in.at[pl.ds(n * strip, strip), pl.ds(0, 3 * heads_width)]
        return pltpu.make_async_copy(src, qkv_w.at[n % 2], strip_sem.at[n % 2])

    late_load = pltpu.make_async_copy(turned_in, turned, load_sem.at[1])
    lane = lax.broadcasted_iota(jnp.int32, (tokens, head), 1)
    sign = jnp.where(lane < head // 2, -1.0, 1.0)

    def unrotated(grads):
        turned_part = pltpu.roll(grads * sin_in[...], head // 2, 1) * sign
        return grads * cos_in[...] - turned_part

    def attention(d_low, out_w, q_all, k_all, v_all, d_att, probs, d_probs):
        pairs = (
            (d_low_in, d_low),
            (weights_in.at[:, pl.ds(3 * heads_width, heads_width)], out_w),
            (q_in, q_all),
            (k_in, k_all),
            (v_in, v_all),
        )
        copies = [
            pltpu.make_async_copy(src, dst, load_sem.at[2 + i])
            for i, (src, dst) in enumerate(pairs)
        ]
        for copy in copies + [late_load, load_strip(0), load_strip(1)]:
            copy.start()
        at.greet_row()
        rows_begin(0)
        copies[0].wait()
        copies[1].wait()
        d_attended = jnp.dot(d_low[...], out_w[...], preferred_element_type=f32).astype(bf16)
        for h in range(heads):
            d_att[h] = d_attended[:, h * head : (h + 1) * head]
        for copy in copies[2:]:
            copy.wait()

        def head_body(h, carry):
            queries, d_a = q_all[h], d_att[h]
            delta = jnp.zeros((1, tokens), f32)
            for w in range(windows):
                some = slice(w * tokens, (w + 1) * tokens)
                scores = lax.dot_general(
                    k_all[h, some], queries, across, preferred_element_type=f32
                )
                key_at = lax.broadcasted_iota(jnp.int32, scores.shape, 0)
                key_at = key_at + (at.ep + w + 1 - windows) * tokens
                allowed = (key_at >= query_start[...]) & (key_at <= query_at[...])
                p = jnp.where(allowed, jnp.exp(scores * score_scale - lse_in[h]), 0.0)
                d_p = lax.dot_general(v_all[h, some], d_a, across, preferred_element_type=f32)
                probs[w] = p
                d_probs[w] = d_p
                delta = delta + jnp.sum(p * d_p, axis=0, keepdims=True)
            d_queries = jnp.zeros((head, tokens), f32)
            for w in range(windows):
                some = slice(w * tokens, (w + 1) * tokens)
                p = probs[w]
                d_scores = (p * (d_probs[w] - delta)).astype(bf16)
                d_keys = jnp.dot(d_scores, queries, preferred_element_type=f32) * score_scale
                d_values = jnp.dot(p.astype(bf16), d_a, preferred_element_type=f32)
                if w < windows - 1:
                    d_out[w, h, :, :head] = d_keys.astype(bf16)
                    d_out[w, h, :, head:] = d_values.astype(bf16)

                    @pl.when(at.ep >= 2 - w)
                    def _():
                        d_copy(w, h).start()

                else:
                    d_own[h, :, :head] = d_keys
                    d_own[h, :, head:] = d_values
                d_queries = d_queries + jnp.dot(
                    k_all[h, some].T, d_scores, preferred_element_type=f32
                )
            here = pl.ds(pl.multiple_of(h * head, head), head)
            d_proj[:, here] = unrotated((d_queries * score_scale).T).astype(bf16)
            return carry

        lax.fori_loop(0, heads, head_body, 0)

    pl.run_scoped(
        attention,
        pltpu.VMEM((tokens, width), bf16),
        pltpu.VMEM((width, heads_width), bf16),
        pltpu.VMEM((heads, tokens, head), bf16),
        pltpu.VMEM((heads, windows * tokens, head), bf16),
        pltpu.VMEM((heads, windows * tokens, head), bf16),
        pltpu.VMEM((heads, tokens, head), bf16),
        pltpu.VMEM((windows, tokens, tokens), f32),
        pltpu.VMEM((windows, tokens, tokens), f32),
    )
    order = [j for j in range(1, depth)] + [0]

    def own_body(h, carry):
        for w in range(windows - 1):

            @pl.when(at.ep + (2 - w) < count)
            def _():
                d_arrival(w, h).wait_recv()
                d_own[h] += d_got[w, h].astype(f32)

        k_here = pl.ds(pl.multiple_of(heads_width + h * head, head), head)
        v_here = pl.ds(pl.multiple_of(2 * heads_width + h * head, head), head)
        d_proj[:, k_here] = unrotated(d_own[h, :, :head]).astype(bf16)
        d_proj[:, v_here] = d_own[h, :, head:].astype(bf16)
        return carry

    def weight_rows(into, q, z, y):
        here = pl.ds(pl.multiple_of((z * 2 + y) * rows, rows), rows)
        product = jnp.dot(turned[here], d_proj[:, cuts[q]], preferred_element_type=f32)
        into[:, cuts[q]] = product.astype(bf16)

    def begin_sums(q):
        for j in order:
            weight_rows(y_out.at[j], q, at.ahead(j), 1 - at.y)
            y_copy(q, j).start()

    def own_sums(q):
        for j in order:
            weight_rows(own.at[j], q, at.ahead(j), at.y)

    def projections():
        lax.fori_loop(0, heads, own_body, 0)
        for n in range(strips):
            some = slice(n * strip, (n + 1) * strip)
            load_strip(n).wait()
            product = lax.dot_general(
                d_proj[...], qkv_w[n % 2], across, preferred_element_type=f32
            )
            part[:, :, :, some] = product.astype(bf16).reshape(2, 2, quarter, strip)
            if n + 2 < strips:
                load_strip(n + 2).start()
        core_copy().start()
        begin_sums(1)
        core_copy().wait()
        for x in (0, 1):
            part[x, at.c] = part[x, at.c] + core_got[x]
        x_copy().start()
        own_sums(1)
        x_copy().wait()

        def end_body(i, carry):
            here = pl.ds(pl.multiple_of(i * few, few), few)
            grads = part[at.x, at.c, here].astype(f32) + x_got[here].astype(f32)
            inputs = own_rows_in[here].astype(f32)
            scale = lax.rsqrt(jnp.mean(inputs * inputs, axis=1, keepdims=True) + epsilon)
            unit_rows = inputs * scale
            scaled = grads * gain_in[...]
            inner = jnp.mean(scaled * unit_rows, axis=1, keepdims=True)
            total = d_resid_in[here] + scale * (scaled - unit_rows * inner)
            d_rows[here] = total.astype(bf16)
            return carry + jnp.sum(grads * unit_rows, axis=0, keepdims=True)

        d_gain = lax.fori_loop(0, quarter // few, end_body, jnp.zeros((1, width), f32))
        rows_begin(1)
        line = lax.broadcasted_iota(jnp.int32, (128, rows), 0)
        for e in range(count):
            some = slice(e * rows, (e + 1) * rows)
            gains = jnp.where(line == 0, d_gain[:, some], 0.0)
            gains = jnp.where(line == 1, gain_two_in[:, some], gains)
            small_own[e // 2, e % 2] = (gains.T + side_in[some]).astype(bf16)
        for j in order:
            little_y(j).start()

    def after_y(q, j):
        y_copy(q, j).wait_recv()

        def body(i, carry):
            some = pl.ds(pl.multiple_of(i * few, few), few)
            own[j, some, cuts[q]] = own[j, some, cuts[q]] + hop[j, some, cuts[q]]
            return carry

        lax.fori_loop(0, rows // few, body, 0)
        if j > 0:
            z_copy(q, j).start()

    def after_little():
        for j in order:
            little_y(j).wait_recv()
            here = small_own.at[at.ahead(j), at.y]
            here[...] = here[...] + small_hop[j]
            if j > 0:
                little_z(j).start()

    hooks = {(0, 0): [functools.partial(rows_pass_on, 0)]}
    for i, j in enumerate(order):
        hooks.setdefault((0, min(2 * i + 1, count - 1)), []).append(functools.partial(after_y, 0, j))
    hooks[(1, 2)] = [functools.partial(rows_pass_on, 1)]
    hooks[(1, 3)] = [after_little]
    last_hooks = []
    for i, j in enumerate(order):
        when = count + 5 + 5 * i
        due = functools.partial(after_y, 1, j)
        if when < 3 * count:
            hooks.setdefault((when // count, when % count), []).append(due)
        else:
            last_hooks.append(due)

    def weight_gradients(turned_left, left_tile, right_part, staging):
        lefts = (
            lambda tile: d_pair_in.at[tile, :, pl.ds(0, hidden)],
            lambda tile: d_pair_in.at[tile, :, pl.ds(hidden, hidden)],
            lambda tile: weighted_in.at[tile],
        )
        rights = (rows_in, rows_in, upstream_in)
        results = (gate_out, up_out, down_out)
        columns = width // count

        def load_left(p, tile):
            slot = lax.rem(tile, 2)
            return pltpu.make_async_copy(
                lefts[p](tile), left_tile.at[slot], tile_sem.at[0, slot]
            )

        def load_right(p, n):
            slot = lax.rem(n, 2)
            here = pl.ds(pl.multiple_of(n * columns, columns), columns)
            return pltpu.make_async_copy(
                rights[p].at[:, :, here], right_part.at[slot], tile_sem.at[1, slot]
            )

        def store(p, n):
            slot = lax.rem(n, 2)
            here = pl.ds(pl.multiple_of(n * columns, columns), columns)
            return pltpu.make_async_copy(
                staging.at[slot], results[p].at[:, here], store_sem.at[slot]
            )

        def turn_left(p, tile):
            load_left(p, tile).wait()

            @pl.when(tile + 1 < count)
            def _():
                load_left(p, tile + 1).start()

            here = pl.ds(pl.multiple_of(tile * tokens, tokens), tokens)
            turned_left[:, here] = left_tile[lax.rem(tile, 2)].T

        def run_pass(p):
            def part_body(n, carry):
                slot = lax.rem(n, 2)
                load_right(p, n).wait()

                @pl.when(n + 1 < count)
                def _():
                    load_right(p, n + 1).start()

                if p < 2:

                    @pl.when(n + 1 == count)
                    def _():
                        load_right(p + 1, 0).start()

                @pl.when(n >= 2)
                def _():
                    store(p, n - 2).wait()

                product = jnp.dot(
                    turned_left[...],
                    right_part[slot].reshape(count * tokens, columns),
                    preferred_element_type=f32,
                )
                staging[slot] = product[:routed].astype(bf16)
                pieces[n, p * shared_hidden : (p + 1) * shared_hidden] = product[
                    routed : routed + shared_hidden
                ].astype(bf16)
                store(p, n).start()
                for (hook_pass, hook_part), actions in hooks.items():
                    if hook_pass == p:

                        @pl.when(n == hook_part)
                        def _():
                            for action in actions:
                                action()

                return carry

            def turn_body(tile, carry):
                turn_left(p, tile)
                return carry

            lax.fori_loop(0, count, turn_body, 0)
            if p < 2:
                load_left(p + 1, 0).start()
            lax.fori_loop(0, count, part_body, 0)
            for n in (count - 2, count - 1):
                store(p, n).wait()
            swap_own(p).start()
            for copy in swap_copies(p, True):
                copy.start()

        load_left(0, 0).start()
        load_right(0, 0).start()
        late_load.wait()
        begin_sums(0)
        own_sums(0)

        run_pass(0)
        projections()
        run_pass(1)
        run_pass(2)
        for action in last_hooks:
            action()

    pl.run_scoped(
        weight_gradients,
        pltpu.VMEM((hidden, count * tokens), bf16),
        pltpu.VMEM((2, tokens, hidden), bf16),
        pltpu.VMEM((2, count, tokens, width // count), bf16),
        pltpu.VMEM((2, routed, width // count), bf16),
    )
    total = small_own[at.z, at.y].astype(f32)
    for j in range(1, depth):
        little_z(j).wait_recv()
        total = total + small_z[j - 1].astype(f32)
    for kind in (0, 1):
        small[kind] = total
        small_copy(kind).start()
        small_copy(kind).wait()
        total = small[kind] + small_got[kind]
    small_out[...] = total
    for j in range(1, depth):
        for q in (0, 1):
            z_copy(q, j).wait_recv()

    def total_body(i, carry):
        some = pl.ds(pl.multiple_of(i * few, few), few)
        result = own[0, some].astype(f32)
        for k in range(depth - 1):
            result = result + from_z[k, some].astype(f32)
        out[some] = result
        return carry

    lax.fori_loop(0, rows // few, total_body, 0)
    for j in range(depth):
        little_y(j).wait_send()
        if j > 0:
            little_z(j).wait_send()
        for q in (0, 1):
            y_copy(q, j).wait_send()
            if j > 0:
                z_copy(q, j).wait_send()
    for a in (0, 1):
        rows_end(a)
    for p in range(3):
        swap_own(p).wait()
        for copy in swap_copies(p, False):
            copy.wait_recv()
        for copy in swap_copies(p, True):
            copy.wait_send()

    def finish(h, carry):
        for w in range(windows - 1):

            @pl.when(at.ep >= 2 - w)
            def _():
                d_copy(w, h).wait_send()

        return carry

    lax.fori_loop(0, heads, finish, 0)


def backward(large, tiles_of, in_place, units, scale):
    d_low, _, queries, keys = large[:4]
    heads, tokens, head = queries.shape
    width = d_low.shape[1]
    ep_count = lax.axis_size("ep")
    depth, rows = ep_count // 2, width // ep_count
    quarter = tokens // lax.axis_size("tp")
    windows = keys.shape[1] // tokens
    columns = 3 * heads * head
    hidden = tiles_of[3].shape[2]
    slot_here, slot_hidden, shared_hidden = units
    f32, bf16 = jnp.float32, jnp.bfloat16
    anywhere = pl.BlockSpec(memory_space=pl.ANY)
    in_vmem = pl.BlockSpec(memory_space=pltpu.VMEM)
    dma = pltpu.SemaphoreType.DMA
    pieces = (ep_count, 3 * shared_hidden, rows)
    gathered = jax.ShapeDtypeStruct((2, 2, quarter, width), bf16)
    routed = jax.ShapeDtypeStruct((slot_here * slot_hidden, width), bf16)

    def vmem(*shape, dtype=bf16):
        return pltpu.VMEM(shape, dtype)

    out, small, block_out, d_rows, pieces, gate, up, down = pl.pallas_call(
        functools.partial(back_kernel, units, scale),
        out_shape=(
            jax.ShapeDtypeStruct((rows, columns), f32),
            jax.ShapeDtypeStruct((rows, 128), f32),
            gathered,
            gathered,
            jax.ShapeDtypeStruct(pieces, bf16),
            routed,
            routed,
            routed,
        ),
        in_specs=[anywhere] * (len(large) + len(tiles_of)) + [in_vmem] * len(in_place),
        out_specs=(in_vmem, in_vmem) + (anywhere,) * 6,
        scratch_shapes=[
            vmem(2, width // 4, columns),
            vmem(width, tokens),
            vmem(windows - 1, heads, tokens, 2 * head),
            vmem(windows - 1, heads, tokens, 2 * head),
            vmem(heads, tokens, 2 * head, dtype=f32),
            vmem(tokens, columns),
            vmem(2, 2, quarter, width),
            vmem(2, quarter, width),
            vmem(quarter, width),
            vmem(quarter, width),
            vmem(depth, rows, columns),
            vmem(depth, rows, columns),
            vmem(depth, rows, columns),
            vmem(depth - 1, rows, columns),
            vmem(depth, 2, rows, 128),
            vmem(depth, rows, 128),
            vmem(depth - 1, rows, 128),
            vmem(2, rows, 128, dtype=f32),
            vmem(2, rows, 128, dtype=f32),
            vmem(*pieces),
            dma((7,)),
            dma((windows - 1, heads)),
            dma((windows - 1, heads)),
            dma((2,)),
            dma((2,)),
            dma((2, depth)),
            dma((2, depth)),
            dma((2, depth)),
            dma((2, depth)),
            dma((2, depth)),
            dma((2, depth)),
            dma((2,)),
            dma((2,)),
            dma((3, ep_count)),
            dma((3, ep_count)),
            dma((2, 3)),
            dma((2, 3)),
            dma((5,)),
            dma((2, 2)),
            dma((2,)),
            dma((2,)),
        ],
        compiler_params=pltpu.CompilerParams(
            collective_id=4, has_side_effects=True, vmem_limit_bytes=62 * 2**20
        ),
        cost_estimate=pl.CostEstimate(
            flops=6 * ep_count * tokens * width * hidden,
            bytes_accessed=8 * ep_count * tokens * width,
            transcendentals=heads * tokens * windows * tokens,
        ),
        name="backward",
    )(*large, *tiles_of, *in_place)
    block_out, d_rows = [array.reshape(4 * quarter, width) for array in (block_out, d_rows)]
    return out, small, block_out, d_rows, pieces, (gate, up, down)


def shared_pieces(weights, ep_count):
    rows, hidden = weights[0].shape
    units = hidden // ep_count
    return jnp.concatenate([weight.T.reshape(ep_count, units, rows) for weight in weights], axis=1)


def shared_whole(pieces, count):
    ep_count, units, columns = pieces.shape
    units = units // count
    pieces = pieces.reshape(ep_count, count, units, columns).astype(jnp.float32)
    return [pieces[:, i].reshape(ep_count * units, columns).T for i in range(count)]


def dense_body(
    tokens,
    lengths,
    routes,
    attn_gain,
    w_query,
    w_key,
    w_value,
    w_out,
    ffn_gain,
    w_router,
    shared_mix,
    shared_gate,
    shared_up,
    shared_down,
    expert_gate,
    expert_up,
    expert_down,
    cotangent,
):
    rows_here, width = tokens.shape
    ep_count = lax.axis_size("ep")
    tp_count = lax.axis_size("tp")
    ep_index = lax.axis_index("ep")
    offset = ep_index * rows_here
    quarter = rows_here // tp_count
    first_row = lax.axis_index("tp") * quarter
    slot_here, slot_hidden = expert_gate.shape[0], expert_gate.shape[1]
    expert_count = w_router.shape[1]
    bf16, f32 = jnp.bfloat16, jnp.float32

    def my_rows(array):
        return lax.dynamic_slice_in_dim(array, first_row, quarter, 0)

    side_columns = jnp.concatenate(
        [attn_gain[:, None], ffn_gain[:, None], shared_mix[:, None], w_router], axis=1
    )
    side_columns = jnp.pad(side_columns, ((0, 0), (0, -side_columns.shape[1] % 128)))
    joined_weights, pieces = gather_over_ep(
        jnp.concatenate([w_query, w_key, w_value, w_out, side_columns], axis=1),
        shared_pieces((shared_gate, shared_up, shared_down), ep_count),
    )
    heads_width = w_query.shape[1]
    side_weight = joined_weights[:, 4 * heads_width :]
    picked = jnp.any(
        my_rows(routes)[:, :, None] == jnp.arange(expert_count, dtype=jnp.int32), axis=1
    )
    picked_lanes = jnp.pad(picked.astype(bf16), ((0, 0), (3, 125 - expert_count)))
    upstream_rows = jnp.concatenate([my_rows(cotangent), picked_lanes], axis=1)
    shared_units = pieces.shape[1] // 3
    routed_units = slot_here * slot_hidden
    heads_here = heads_width // HD
    score_scale = HD ** (-0.5)
    first_norm_scale = side_weight[:, 0].astype(f32)
    second_norm_scale = side_weight[:, 1].astype(f32)
    query_at = offset + jnp.arange(rows_here, dtype=jnp.int32)
    _, query_pos = sequence_info(lengths, query_at)
    cosine, sine = rope_tables(query_pos, HD)
    tables = (cosine[:, 0], sine[:, 0], (query_at - query_pos)[None, :], query_at[None, :])
    (
        upstream_all,
        normed_one_turned,
        keys_win,
        values_win,
        queries,
        log_total,
        attended,
        resid,
        normed_two,
    ) = attention_front(
        tokens,
        joined_weights,
        upstream_rows,
        tables + (my_rows(tokens), first_norm_scale[None, :], second_norm_scale[None, :]),
        heads_here,
        score_scale,
    )
    (
        normed_all,
        weighted_h,
        d_pair_pre,
        block_rows,
        d_resid_low,
        d_resid,
        grad_gain_two,
        d_side,
    ) = ffn_over_all(
        normed_two,
        upstream_all,
        (expert_gate, expert_up, expert_down),
        pieces,
        joined_weights,
        resid,
        second_norm_scale[None, :],
        (slot_here, slot_hidden, shared_units),
        expert_count,
    )
    grad_side = jnp.dot(normed_two.astype(f32).T, d_side, precision=highest)
    grad_out = jnp.einsum("td,th->dh", d_resid_low, attended, preferred_element_type=f32)
    grad_out = lax.psum_scatter(
        grad_out.astype(bf16), "ep", scatter_dimension=0, tiled=True
    ).astype(f32)
    tile_shape = (ep_count, rows_here, -1)
    tiles_of = tuple(
        array.reshape(tile_shape) for array in (normed_all, d_pair_pre, upstream_all, weighted_h)
    )
    units = (slot_here, slot_hidden, shared_units)
    column = jnp.arange(128, dtype=jnp.int32)
    large = (
        d_resid_low,
        joined_weights,
        queries,
        keys_win,
        values_win,
        normed_one_turned,
        block_rows,
    )
    in_place = (
        log_total,
        tables[2],
        tables[3],
        tables[0],
        tables[1],
        my_rows(tokens),
        first_norm_scale[None, :],
        d_resid,
        grad_gain_two[None, :],
        jnp.where(column >= 2, grad_side, 0.0),
    )
    grad_weights, small, block_out, grad_tokens, grad_pieces, grad_experts = backward(
        large, tiles_of, in_place, units, score_scale
    )
    grad_shared = shared_whole(grad_pieces, 3)
    grad_tokens = grad_tokens.astype(f32)
    grad_experts = [grad.astype(f32).reshape(expert_gate.shape) for grad in grad_experts]
    parts = [grad_weights[:, i * heads_width : (i + 1) * heads_width] for i in range(3)]
    return (
        block_out,
        grad_tokens,
        small[:, 0],
        parts[0],
        parts[1],
        parts[2],
        grad_out,
        small[:, 1],
        small[:, 3 : 3 + expert_count],
        small[:, 2],
        grad_shared[0],
        grad_shared[1],
        grad_shared[2],
        grad_experts[0],
        grad_experts[1],
        grad_experts[2],
    )


def chosen_body(*arrays):
    rows_here, top_count = arrays[2].shape
    slot_here, expert_count = arrays[14].shape[0], arrays[9].shape[1]
    capacity = rows_here * top_count * 7 // (5 * expert_count)
    grid_of_two = lax.axis_size("ep") % 2 == 0 and lax.axis_size("tp") == 4
    if grid_of_two and rows_here < 2 * slot_here * capacity:
        return dense_body(*arrays)
    return body(*arrays)


def solution(mesh):
    placed = (
        P("ep", None),
        P(),
        P("ep", None),
        P("ep"),
        P("ep", "tp"),
        P("ep", "tp"),
        P("ep", "tp"),
        P("ep", "tp"),
        P("ep"),
        P("ep", None),
        P("ep"),
        P("ep", "tp"),
        P("ep", "tp"),
        P("ep", "tp"),
        P("ep", "tp", None),
        P("ep", "tp", None),
        P("ep", "tp", None),
        P("ep", None),
    )
    return jax.shard_map(
        chosen_body,
        mesh=mesh,
        in_specs=placed,
        out_specs=(
            P("ep", None),
            P("ep", None),
            P("ep"),
            P("ep", "tp"),
            P("ep", "tp"),
            P("ep", "tp"),
            P("ep", "tp"),
            P("ep"),
            P("ep", None),
            P("ep"),
            P("ep", "tp"),
            P("ep", "tp"),
            P("ep", "tp"),
            P("ep", "tp", None),
            P("ep", "tp", None),
            P("ep", "tp", None),
        ),
        check_vma=False,
    )
```

profile of v0, /device:TPU:13, one launch (start us, length us, event | category | flops | bytes accessed | tf_op | source)
XLA Modules:
  0.0 824.7 jit_solution(1548002600526782278)
XLA Ops:
  7.3 0.9 reduce-window.9
  12.3 1.1 fusion
  13.4 1.6 copy.71
  15.6 1.7 constant_dynamic-update-slice_fusion.3
  17.3 1.7 constant_dynamic-update-slice_fusion.2
  18.9 1.7 constant_dynamic-update-slice_fusion.1
  20.6 1.7 constant_dynamic-update-slice_fusion
  22.9 1.5 pad_maximum_fusion.pieces_in
  24.4 123.4 %gather_weights.1 = (bf16[4,2,256,2176]{3,2,1,0:T(8,128)(2,1)}, bf16[8,528,256]{2,1,0:T(8,128)(2,1)}) custom-call(bf16[256,2176]{1,0:T(8,128)(2,1)} %pad_dynamic-update-slice_fusion.own_in, bf16[8,528,256]{2,1,0:T(8,128)(2,1)} %pad_maximum_fusion.pieces_in), custom_call_target="tpu_custom_call" | custom-call | bytes 17825792 | tf_op jit(solution)/shard_map/gather_weights/pallas_call | solution.py:1280
  147.8 1.8 convert_reduce_fusion
  149.6 1.3 constant_dynamic-slice_fusion
  151.0 114.0 %attention_front.1 = (bf16[4,2,2,2,128,2176]{5,4,3,2,1,0:T(8,128)(2,1)}, bf16[2048,512]{1,0:T(8,128)(2,1)}, bf16[4,1536,128]{2,1,0:T(8,128)(2,1)}, bf16[4,1536,1...) custom-call(bf16[512,2048]{1,0:T(8,128)(2,1)} %block_in.1, ...), custom_call_target="tpu_custom_call" | custom-call | flops 4294967296 | bytes 17825792 | tf_op jit(solution)/shard_map/attention_front/pallas_call | solution.py:1621
  265.1 0.8 copy-done.3
  265.9 0.8 copy-done.11
  267.3 293.4 %ffn_all_tokens.1 = (bf16[4,2,2,2,128,2048]{5,4,3,2,1,0:T(8,128)(2,1)}, bf16[4,2,512,896]{3,2,1,0:T(8,128)(2,1)}, bf16[4,2,512,1792]{3,2,1,0:T(8,128)(2,1)}, bf1...) custom-call(bf16[128,2048]{1,0:T(8,128)(2,1)} %copy-done.3, ...), custom_call_target="tpu_custom_call" | custom-call | flops 90194313216 | bytes 83886080 | tf_op jit(solution)/shard_map/ffn_all_tokens/pallas_call | solution.py:1060
  560.7 4.2 convolution_convert_fusion
  564.9 1.0 copy-done.4
  566.0 1.6 convolution_select_fusion.side_in
  567.6 219.2 %backward.1 = (f32[256,1536]{1,0:T(8,128)}, f32[256,128]{1,0:T(8,128)}, bf16[2,2,128,2048]{3,2,1,0:T(8,128)(2,1)}, bf16[2,2,128,2048]{3,2,1,0:T(8,128)(2,1)}, bf...) custom-call(bf16[512,2048]{1,0:T(8,128)(2,1)} %bitcast.85, ...), custom_call_target="tpu_custom_call" | custom-call | flops 45097156608 | bytes 67108864 | tf_op jit(solution)/shard_map/backward/pallas_call | solution.py:2249
  786.8 1.0 slice.46
  788.5 3.2 fusion.3
  791.7 2.9 copy.81
  794.6 1.5 copy.80
  796.1 1.5 copy.79
  797.7 5.3 convert.11
  802.9 3.3 convert.12
  806.2 3.3 convert.13
  809.5 0.8 slice_reduce_fusion
  810.4 1.2 fusion.4
  811.6 2.7 bitcast_convert_fusion
  814.3 1.8 convert_element_type.68
  816.1 1.3 copy.90
  (66 shorter events, 6.7 us)
Async XLA Ops:
  7.2 3.7 copy-start
  7.2 7.8 copy-start.19
  7.2 8.1 copy-start.20
  7.2 807.0 %reduce-scatter.2.cloned.1.call-start = ((), (), s32[]{:S(2)}) async-start(), calls=%async_computation.1 | async-start | bytes 2359296 | tf_op jit(solution)/shard_map/reduce_scatter | solution.py:2432
  7.3 143.7 %copy-start.10 = (s32[1,512]{1,0:T(1,128)}, s32[1,512]{1,0:T(1,128)S(1)}, u32[]{:S(2)}) copy-start(s32[1,512]{1,0:T(1,128)S(1)} %iota_add_fusion.query_at) | copy-start | bytes 6148
  11.0 140.0 %copy-start.9 = (s32[512]{0:T(512)}, s32[512]{0:T(512)S(1)}, u32[]{:S(2)}) copy-start(s32[512]{0:T(512)S(1)} %select_reduce_fusion) | copy-start | bytes 6148
  13.4 137.6 %copy-start.5 = (f32[512,128]{1,0:T(8,128)}, f32[512,128]{1,0:T(8,128)S(1)}, u32[]{:S(2)}) copy-start(f32[512,128]{1,0:T(8,128)S(1)} %get-tuple-element.145.sin_in) | copy-start | bytes 786436
  13.4 137.6 %copy-start.6 = (f32[512,128]{1,0:T(8,128)}, f32[512,128]{1,0:T(8,128)S(1)}, u32[]{:S(2)}) copy-start(f32[512,128]{1,0:T(8,128)S(1)} %get-tuple-element.146.cos_in) | copy-start | bytes 786436
  149.6 115.5 %copy-start.7 = (f32[2048]{0:T(1024)}, f32[2048]{0:T(1024)S(1)}, u32[]{:S(2)}) copy-start(f32[2048]{0:T(1024)S(1)} %get-tuple-element.135) | copy-start | bytes 24580
  149.6 115.5 %copy-start.8 = (f32[2048]{0:T(1024)}, f32[2048]{0:T(1024)S(1)}, u32[]{:S(2)}) copy-start(f32[2048]{0:T(1024)S(1)} %get-tuple-element.134) | copy-start | bytes 24580
  150.9 114.2 %copy-start.2 = (bf16[128,2048]{1,0:T(8,128)(2,1)}, bf16[128,2048]{1,0:T(8,128)(2,1)S(1)}, u32[]{:S(2)}) copy-start(bf16[128,2048]{1,0:T(8,128)(2,1)S(1)} %get-tuple-element.147.tokens_in.own_rows_in) | copy-start | bytes 1572868
  265.1 0.8 copy-start.3
  265.9 0.8 copy-start.11
  266.7 0.6 copy-start.12
  564.9 1.0 copy-start.4
  564.9 1.0 copy-start.21
  797.6 5.3 copy-start.14
  802.9 3.3 copy-start.13
  806.2 3.3 copy-start.16
  806.2 4.2 copy-start.18
  809.5 2.0 copy-start.15
  811.6 4.5 copy-start.17
  816.1 1.3 copy-start.1
Sparse Core Ops, SparseCore 0:
  565.1 93.3 reduce-scatter.1
where the time goes:
time: 838 us; the launch traced here: 825 us
  Pallas kernels  750 us (89%)
  local copies, waits for them, and re-layouts  30.4 us (4%)
  other arithmetic  23.5 us (3%)
  between operations  14.8 us (2%)
    pallas_call x1, Pallas kernels, ffn_over_all(): pl.pallas_call(functools.partial(ffn_kernel, units, expert_count), out_sh...  293 us
    pallas_call x1, Pallas kernels, backward(): pl.pallas_call(functools.partial(back_kernel, units, scale), out_shape=(j...  219 us
    pallas_call x1, Pallas kernels, gather_over_ep(): pl.pallas_call(weights_kernel, out_shape=(jax.ShapeDtypeStruct((depth, 2,...  123 us
    pallas_call x1, Pallas kernels, attention_front(): pl.pallas_call(functools.partial(front_kernel, scale), out_shape=(shape((...  114 us
    unnamed x53, local copies, waits for them, and re-layouts  17.9 us
  transfers between devices with their start and end apart: 1, of which 0 were waited for; matrix products, arithmetic and copies ran while one was open for 4% of the time, Pallas kernels for 27%

commit v1 on v0

--- a/solution.py
+++ b/solution.py
@@ -1334,12 +1334,38 @@
         peer = self.at.at_z(self.at.ahead(k))
         return remote(self.mine, dst, send.at[k - 1], recv.at[k - 1], peer)
 
+    def z_onward(self, j):
+        send, recv = self.z_sems
+        src = self.block(j, self.at.y, self.at.x)
+        peer = self.at.at_z(self.at.z + 1)
+        return remote(src, src, send.at[self.at.depth - 1 + j], recv.at[j], peer)
+
+    def sends(self, k):
+        down = self.at.z + k >= self.at.depth
+        return down | (self.at.z + 1 < self.at.depth) if k == 1 else down
+
+    def goes_on(self, j):
+        return (self.at.z >= j) & (self.at.z + 1 < self.at.depth)
+
+    def z_start(self):
+        for k in range(1, self.at.depth):
+
+            @pl.when(self.sends(k))
+            def _():
+                self.z_copy(k).start()
+
     def begin(self, j):
         if j > 0:
             send, recv = self.z_sems
             dst = self.block(j, self.at.y, self.at.x)
             peer = self.at.at_z(self.at.behind(j))
             remote(dst, dst, send.at[j - 1], recv.at[j - 1], peer).wait_recv()
+            if j + 1 < self.at.depth:
+
+                @pl.when(self.goes_on(j))
+                def _():
+                    self.z_onward(j).start()
+
         for kind in (0, 1, 4):
             self.plane_copy(j, kind).start()
 
@@ -1358,7 +1384,17 @@
 
     def finish(self):
         for k in range(1, self.at.depth):
-            self.z_copy(k).wait_send()
+
+            @pl.when(self.sends(k))
+            def _():
+                self.z_copy(k).wait_send()
+
+            if k + 1 < self.at.depth:
+
+                @pl.when(self.goes_on(k))
+                def _():
+                    self.z_onward(k).wait_send()
+
         for j in range(self.at.depth):
             for kind in range(8):
                 if kind >= 4:
@@ -1453,7 +1489,7 @@
         upstream_in, gather.block(0, at.y, at.x), load_sem.at[len(pairs)]
     )
     own_copy.start()
-    gather.z_copy(1).start()
+    gather.z_start()
     own_copy.wait()
     gather.begin(0)
     loads[0].wait()
@@ -1489,8 +1525,6 @@
             for kind in (0, 1):
                 kv_copy(kind, w).start()
 
-    for k in range(2, depth):
-        gather.z_copy(k).start()
     gather.spread(0)
     queries = jnp.dot(normed[...], qkv_w[:, :heads_width], preferred_element_type=f32)
     for h in range(heads):
@@ -1645,7 +1679,7 @@
             pltpu.VMEM((2, quarter, width), bf16),
             pltpu.VMEM((quarter, width), bf16),
             dma((4,)),
-            dma((depth - 1,)),
+            dma((2 * depth,)),
             dma((depth - 1,)),
             dma((depth, 8)),
             dma((depth, 8)),
@@ -2047,15 +2081,16 @@
 
     hooks = {(0, 0): [functools.partial(rows_pass_on, 0)]}
     for i, j in enumerate(order):
-        hooks.setdefault((0, min(2 * i + 1, count - 1)), []).append(functools.partial(after_y, 0, j))
-    hooks[(1, 2)] = [functools.partial(rows_pass_on, 1)]
-    hooks[(1, 3)] = [after_little]
+        here = (1, min(count // 2 + i, count - 1))
+        hooks.setdefault(here, []).append(functools.partial(after_y, 0, j))
+    hooks[(2, 2)] = [functools.partial(rows_pass_on, 1)]
+    hooks[(2, 3)] = [after_little]
     last_hooks = []
     for i, j in enumerate(order):
-        when = count + 5 + 5 * i
+        when = 2 + 5 * i
         due = functools.partial(after_y, 1, j)
-        if when < 3 * count:
-            hooks.setdefault((when // count, when % count), []).append(due)
+        if when < count:
+            hooks.setdefault((2, when), []).append(due)
         else:
             last_hooks.append(due)
 
@@ -2149,9 +2184,14 @@
             for n in (count - 2, count - 1):
                 store(p, n).wait()
             swap_own(p).start()
+            if p > 0:
+                start_swap(p)
+
+        def start_swap(p):
             for copy in swap_copies(p, True):
                 copy.start()
 
+        hooks.setdefault((1, count - 2), []).append(functools.partial(start_swap, 0))
         load_left(0, 0).start()
         load_right(0, 0).start()
         late_load.wait()
@@ -2159,8 +2199,8 @@
         own_sums(0)
 
         run_pass(0)
+        run_pass(1)
         projections()
-        run_pass(1)
         run_pass(2)
         for action in last_hooks:
             action()

time: 838 us -> 797 us (0.951)
  Pallas kernels: 750 us -> 714 us
    pallas_call x1, Pallas kernels: 293 us -> 269 us  [ffn_over_all(): pl.pallas_call(functools.partial(ffn_kernel, units, expert_count), out_sh...]
    pallas_call x1, Pallas kernels: 219 us -> 208 us  [backward(): pl.pallas_call(functools.partial(back_kernel, units, scale), out_shape=(j...]
  transfers between devices with their start and end apart: 1 -> 1, of which waited for: 0 -> 0; matrix products, arithmetic and copies ran while one was open for 4% -> 4% of each run, Pallas kernels for 27% -> 26%
where the time goes in v1:
time: 797 us; the launch traced here: 789 us
  Pallas kernels  714 us (90%)
  local copies, waits for them, and re-layouts  30.4 us (4%)
  other arithmetic  23.5 us (3%)
  between operations  14.8 us (2%)
    pallas_call x1, Pallas kernels, ffn_over_all(): pl.pallas_call(functools.partial(ffn_kernel, units, expert_count), out_sh...  269 us
    pallas_call x1, Pallas kernels, backward(): pl.pallas_call(functools.partial(back_kernel, units, scale), out_shape=(j...  208 us
    pallas_call x1, Pallas kernels, gather_over_ep(): pl.pallas_call(weights_kernel, out_shape=(jax.ShapeDtypeStruct((depth, 2,...  123 us
    pallas_call x1, Pallas kernels, attention_front(): pl.pallas_call(functools.partial(front_kernel, scale), out_shape=(shape((...  114 us
    unnamed x53, local copies, waits for them, and re-layouts  17.9 us
  transfers between devices with their start and end apart: 1, of which 0 were waited for; matrix products, arithmetic and copies ran while one was open for 4% of the time, Pallas kernels for 26%

profile of v1, /device:TPU:13, one launch (start us, length us, event | category | flops | bytes accessed | tf_op | source)
XLA Modules:
  0.0 788.8 jit_solution(897765311705376844)
XLA Ops:
  7.3 0.9 reduce-window.9
  12.3 1.1 fusion
  13.4 1.6 copy.71
  15.6 1.7 constant_dynamic-update-slice_fusion.3
  17.3 1.7 constant_dynamic-update-slice_fusion.2
  18.9 1.7 constant_dynamic-update-slice_fusion.1
  20.6 1.7 constant_dynamic-update-slice_fusion
  22.9 1.5 pad_maximum_fusion.pieces_in
  24.4 123.4 %gather_weights.1 = (bf16[4,2,256,2176]{3,2,1,0:T(8,128)(2,1)}, bf16[8,528,256]{2,1,0:T(8,128)(2,1)}) custom-call(bf16[256,2176]{1,0:T(8,128)(2,1)} %pad_dynamic-update-slice_fusion.own_in, bf16[8,528,256]{2,1,0:T(8,128)(2,1)} %pad_maximum_fusion.pieces_in), custom_call_target="tpu_custom_call" | custom-call | bytes 17825792 | tf_op jit(solution)/shard_map/gather_weights/pallas_call | solution.py:1280
  147.8 1.8 convert_reduce_fusion
  149.6 1.3 constant_dynamic-slice_fusion
  151.0 113.8 %attention_front.1 = (bf16[4,2,2,2,128,2176]{5,4,3,2,1,0:T(8,128)(2,1)}, bf16[2048,512]{1,0:T(8,128)(2,1)}, bf16[4,1536,128]{2,1,0:T(8,128)(2,1)}, bf16[4,1536,1...) custom-call(bf16[512,2048]{1,0:T(8,128)(2,1)} %block_in.1, ...), custom_call_target="tpu_custom_call" | custom-call | flops 4294967296 | bytes 17825792 | tf_op jit(solution)/shard_map/attention_front/pallas_call | solution.py:1655
  264.9 0.8 copy-done.3
  265.7 0.8 copy-done.11
  267.1 269.0 %ffn_all_tokens.1 = (bf16[4,2,2,2,128,2048]{5,4,3,2,1,0:T(8,128)(2,1)}, bf16[4,2,512,896]{3,2,1,0:T(8,128)(2,1)}, bf16[4,2,512,1792]{3,2,1,0:T(8,128)(2,1)}, bf1...) custom-call(bf16[128,2048]{1,0:T(8,128)(2,1)} %copy-done.3, ...), custom_call_target="tpu_custom_call" | custom-call | flops 90194313216 | bytes 83886080 | tf_op jit(solution)/shard_map/ffn_all_tokens/pallas_call | solution.py:1060
  536.1 4.2 convolution_convert_fusion
  540.3 1.0 copy-done.4
  541.3 1.6 convolution_select_fusion.side_in
  543.0 207.9 %backward.1 = (f32[256,1536]{1,0:T(8,128)}, f32[256,128]{1,0:T(8,128)}, bf16[2,2,128,2048]{3,2,1,0:T(8,128)(2,1)}, bf16[2,2,128,2048]{3,2,1,0:T(8,128)(2,1)}, bf...) custom-call(bf16[512,2048]{1,0:T(8,128)(2,1)} %bitcast.85, ...), custom_call_target="tpu_custom_call" | custom-call | flops 45097156608 | bytes 67108864 | tf_op jit(solution)/shard_map/backward/pallas_call | solution.py:2289
  750.9 1.0 slice.46
  752.6 3.2 fusion.3
  755.8 2.9 copy.81
  758.7 1.5 copy.80
  760.2 1.5 copy.79
  761.7 5.3 convert.11
  767.0 3.3 convert.12
  770.3 3.3 convert.13
  773.6 0.8 slice_reduce_fusion
  774.5 1.2 fusion.4
  775.7 2.7 bitcast_convert_fusion
  778.4 1.8 convert_element_type.68
  780.2 1.3 copy.90
  (66 shorter events, 6.7 us)
Async XLA Ops:
  7.2 3.7 copy-start
  7.2 7.8 copy-start.19
  7.2 8.1 %copy-start.20 = (bf16[256,1408]{1,0:T(8,128)(2,1)S(1)}, bf16[256,1408]{1,0:T(8,128)(2,1)}, u32[]{:S(2)}) copy-start(bf16[256,1408]{1,0:T(8,128)(2,1)} %param.31) | copy-start | bytes 2162692
  7.2 771.1 %reduce-scatter.2.cloned.1.call-start = ((), (), s32[]{:S(2)}) async-start(), calls=%async_computation.1 | async-start | bytes 2359296 | tf_op jit(solution)/shard_map/reduce_scatter | solution.py:2472
  7.3 143.7 %copy-start.10 = (s32[1,512]{1,0:T(1,128)}, s32[1,512]{1,0:T(1,128)S(1)}, u32[]{:S(2)}) copy-start(s32[1,512]{1,0:T(1,128)S(1)} %iota_add_fusion.query_at) | copy-start | bytes 6148
  11.0 140.0 %copy-start.9 = (s32[512]{0:T(512)}, s32[512]{0:T(512)S(1)}, u32[]{:S(2)}) copy-start(s32[512]{0:T(512)S(1)} %select_reduce_fusion) | copy-start | bytes 6148
  13.4 137.6 %copy-start.5 = (f32[512,128]{1,0:T(8,128)}, f32[512,128]{1,0:T(8,128)S(1)}, u32[]{:S(2)}) copy-start(f32[512,128]{1,0:T(8,128)S(1)} %get-tuple-element.145.sin_in) | copy-start | bytes 786436
  13.4 137.6 %copy-start.6 = (f32[512,128]{1,0:T(8,128)}, f32[512,128]{1,0:T(8,128)S(1)}, u32[]{:S(2)}) copy-start(f32[512,128]{1,0:T(8,128)S(1)} %get-tuple-element.146.cos_in) | copy-start | bytes 786436
  149.6 115.2 %copy-start.7 = (f32[2048]{0:T(1024)}, f32[2048]{0:T(1024)S(1)}, u32[]{:S(2)}) copy-start(f32[2048]{0:T(1024)S(1)} %get-tuple-element.135) | copy-start | bytes 24580
  149.6 115.2 %copy-start.8 = (f32[2048]{0:T(1024)}, f32[2048]{0:T(1024)S(1)}, u32[]{:S(2)}) copy-start(f32[2048]{0:T(1024)S(1)} %get-tuple-element.134) | copy-start | bytes 24580
  150.9 113.9 %copy-start.2 = (bf16[128,2048]{1,0:T(8,128)(2,1)}, bf16[128,2048]{1,0:T(8,128)(2,1)S(1)}, u32[]{:S(2)}) copy-start(bf16[128,2048]{1,0:T(8,128)(2,1)S(1)} %get-tuple-element.147.tokens_in.own_rows_in) | copy-start | bytes 1572868
  264.9 0.8 copy-start.3
  265.7 0.8 copy-start.11
  266.5 0.6 copy-start.12
  540.3 1.0 copy-start.4
  540.3 1.0 copy-start.21
  761.7 5.3 copy-start.14
  767.0 3.3 copy-start.13
  770.3 3.3 copy-start.16
  770.3 4.2 copy-start.18
  773.6 2.0 copy-start.15
  775.7 4.5 copy-start.17
  780.2 1.3 copy-start.1
Sparse Core Ops, SparseCore 0:
  540.4 102.5 reduce-scatter.1

commit v2 on v1

--- a/solution.py
+++ b/solution.py
@@ -1813,13 +1813,20 @@
         )
 
     def z_copy(q, j):
+        down = (at.z + j) // depth
+        upper, lower = depth if j == 1 else j - 1, 0 if j == depth - 1 else j + 1
+        slot = upper + down * (lower - upper)
         return remote(
             own.at[j, :, cuts[q]],
-            from_z.at[j - 1, :, cuts[q]],
+            from_z.at[slot, :, cuts[q]],
             z_send.at[q, j],
-            z_recv.at[q, j],
-            at.at_z(at.ahead(j)),
+            z_recv.at[q, slot],
+            at.at_z(at.z + 1 - 2 * down),
         )
+
+    def z_arrival(q, slot):
+        dst = from_z.at[slot, :, cuts[q]]
+        return remote(dst, dst, z_send.at[q, 0], z_recv.at[q, slot], at.next_y)
 
     def little_y(j):
         return remote(
@@ -1986,7 +1993,7 @@
         pltpu.VMEM((windows, tokens, tokens), f32),
         pltpu.VMEM((windows, tokens, tokens), f32),
     )
-    order = [j for j in range(1, depth)] + [0]
+    order = [j for j in range(depth - 1, 0, -1)] + [0]
 
     def own_body(h, carry):
         for w in range(windows - 1):
@@ -2059,17 +2066,31 @@
         for j in order:
             little_y(j).start()
 
+    def add_rows(q, j, other):
+        def body(i, carry):
+            some = pl.ds(pl.multiple_of(i * few, few), few)
+            own[j, some, cuts[q]] = own[j, some, cuts[q]] + other[j, some, cuts[q]]
+            return carry
+
+        lax.fori_loop(0, rows // few, body, 0)
+
+    def pass_on(q, turn, slots):
+        for j in slots:
+            down = (at.z + j) // depth
+            before = down * (depth - 1 - at.z) + (1 - down) * at.z
+
+            @pl.when(before == turn)
+            def _():
+                if turn > 0:
+                    z_arrival(q, j).wait_recv()
+                    add_rows(q, j, from_z)
+                z_copy(q, j).start()
+
     def after_y(q, j):
         y_copy(q, j).wait_recv()
-
-        def body(i, carry):
-            some = pl.ds(pl.multiple_of(i * few, few), few)
-            own[j, some, cuts[q]] = own[j, some, cuts[q]] + hop[j, some, cuts[q]]
-            return carry
-
-        lax.fori_loop(0, rows // few, body, 0)
+        add_rows(q, j, hop)
         if j > 0:
-            z_copy(q, j).start()
+            pass_on(q, 0, [j])
 
     def after_little():
         for j in order:
@@ -2085,6 +2106,9 @@
         hooks.setdefault(here, []).append(functools.partial(after_y, 0, j))
     hooks[(2, 2)] = [functools.partial(rows_pass_on, 1)]
     hooks[(2, 3)] = [after_little]
+    for turn in range(1, depth - 1):
+        here = (2, min(4 * (turn - 1), count - 1))
+        hooks.setdefault(here, []).append(functools.partial(pass_on, 0, turn, order[:-1]))
     last_hooks = []
     for i, j in enumerate(order):
         when = 2 + 5 * i
@@ -2204,6 +2228,8 @@
         run_pass(2)
         for action in last_hooks:
             action()
+        for turn in range(1, depth - 1):
+            pass_on(1, turn, order[:-1])
 
     pl.run_scoped(
         weight_gradients,
@@ -2222,19 +2248,27 @@
         small_copy(kind).wait()
         total = small[kind] + small_got[kind]
     small_out[...] = total
-    for j in range(1, depth):
-        for q in (0, 1):
-            z_copy(q, j).wait_recv()
 
     def total_body(i, carry):
         some = pl.ds(pl.multiple_of(i * few, few), few)
-        result = own[0, some].astype(f32)
-        for k in range(depth - 1):
-            result = result + from_z[k, some].astype(f32)
-        out[some] = result
+        out[some] = own[0, some].astype(f32)
         return carry
 
     lax.fori_loop(0, rows // few, total_body, 0)
+
+    def add_arrived(slot):
+        for q in (0, 1):
+            z_arrival(q, slot).wait_recv()
+
+        def body(i, carry):
+            some = pl.ds(pl.multiple_of(i * few, few), few)
+            out[some] += from_z[slot, some].astype(f32)
+            return carry
+
+        lax.fori_loop(0, rows // few, body, 0)
+
+    pl.when(at.z + 1 < depth)(lambda: add_arrived(0))
+    pl.when(at.z > 0)(lambda: add_arrived(depth))
     for j in range(depth):
         little_y(j).wait_send()
         if j > 0:
@@ -2314,7 +2348,7 @@
             vmem(depth, rows, columns),
             vmem(depth, rows, columns),
             vmem(depth, rows, columns),
-            vmem(depth - 1, rows, columns),
+            vmem(depth + 1, rows, columns),
             vmem(depth, 2, rows, 128),
             vmem(depth, rows, 128),
             vmem(depth - 1, rows, 128),
@@ -2329,7 +2363,7 @@
             dma((2, depth)),
             dma((2, depth)),
             dma((2, depth)),
-            dma((2, depth)),
+            dma((2, depth + 1)),
             dma((2, depth)),
             dma((2, depth)),
             dma((2,)),

time: 797 us -> 807 us (1.013)
  transfers between devices with their start and end apart: 1 -> 1, of which waited for: 0 -> 0; matrix products, arithmetic and copies ran while one was open for 4% -> 4% of each run, Pallas kernels for 26% -> 27%
where the time goes in v2:
time: 807 us; the launch traced here: 791 us
  Pallas kernels  716 us (89%)
  local copies, waits for them, and re-layouts  30.4 us (4%)
  other arithmetic  23.5 us (3%)
  between operations  14.8 us (2%)
    pallas_call x1, Pallas kernels, ffn_over_all(): pl.pallas_call(functools.partial(ffn_kernel, units, expert_count), out_sh...  269 us
    pallas_call x1, Pallas kernels, backward(): pl.pallas_call(functools.partial(back_kernel, units, scale), out_shape=(j...  210 us
    pallas_call x1, Pallas kernels, gather_over_ep(): pl.pallas_call(weights_kernel, out_shape=(jax.ShapeDtypeStruct((depth, 2,...  123 us
    pallas_call x1, Pallas kernels, attention_front(): pl.pallas_call(functools.partial(front_kernel, scale), out_shape=(shape((...  114 us
    unnamed x53, local copies, waits for them, and re-layouts  17.9 us
  transfers between devices with their start and end apart: 1, of which 0 were waited for; matrix products, arithmetic and copies ran while one was open for 4% of the time, Pallas kernels for 27%

profile of v2, /device:TPU:13, one launch (start us, length us, event | category | flops | bytes accessed | tf_op | source)
XLA Modules:
  0.0 791.0 jit_solution(15679047905132854356)
XLA Ops:
  7.3 0.9 reduce-window.9
  12.3 1.1 fusion
  13.4 1.6 copy.71
  15.6 1.7 constant_dynamic-update-slice_fusion.3
  17.3 1.7 constant_dynamic-update-slice_fusion.2
  18.9 1.7 constant_dynamic-update-slice_fusion.1
  20.6 1.7 constant_dynamic-update-slice_fusion
  22.9 1.5 pad_maximum_fusion.pieces_in
  24.4 123.4 %gather_weights.1 = (bf16[4,2,256,2176]{3,2,1,0:T(8,128)(2,1)}, bf16[8,528,256]{2,1,0:T(8,128)(2,1)}) custom-call(bf16[256,2176]{1,0:T(8,128)(2,1)} %pad_dynamic-update-slice_fusion.own_in, bf16[8,528,256]{2,1,0:T(8,128)(2,1)} %pad_maximum_fusion.pieces_in), custom_call_target="tpu_custom_call" | custom-call | bytes 17825792 | tf_op jit(solution)/shard_map/gather_weights/pallas_call | solution.py:1280
  147.8 1.8 convert_reduce_fusion
  149.6 1.3 constant_dynamic-slice_fusion
  151.0 113.8 %attention_front.1 = (bf16[4,2,2,2,128,2176]{5,4,3,2,1,0:T(8,128)(2,1)}, bf16[2048,512]{1,0:T(8,128)(2,1)}, bf16[4,1536,128]{2,1,0:T(8,128)(2,1)}, bf16[4,1536,1...) custom-call(bf16[512,2048]{1,0:T(8,128)(2,1)} %block_in.1, ...), custom_call_target="tpu_custom_call" | custom-call | flops 4294967296 | bytes 17825792 | tf_op jit(solution)/shard_map/attention_front/pallas_call | solution.py:1655
  264.9 0.8 copy-done.3
  265.7 0.8 copy-done.11
  267.1 269.0 %ffn_all_tokens.1 = (bf16[4,2,2,2,128,2048]{5,4,3,2,1,0:T(8,128)(2,1)}, bf16[4,2,512,896]{3,2,1,0:T(8,128)(2,1)}, bf16[4,2,512,1792]{3,2,1,0:T(8,128)(2,1)}, bf1...) custom-call(bf16[128,2048]{1,0:T(8,128)(2,1)} %copy-done.3, ...), custom_call_target="tpu_custom_call" | custom-call | flops 90194313216 | bytes 83886080 | tf_op jit(solution)/shard_map/ffn_all_tokens/pallas_call | solution.py:1060
  536.1 4.2 convolution_convert_fusion
  540.3 1.0 copy-done.4
  541.3 1.6 convolution_select_fusion.side_in
  543.0 210.1 %backward.1 = (f32[256,1536]{1,0:T(8,128)}, f32[256,128]{1,0:T(8,128)}, bf16[2,2,128,2048]{3,2,1,0:T(8,128)(2,1)}, bf16[2,2,128,2048]{3,2,1,0:T(8,128)(2,1)}, bf...) custom-call(bf16[512,2048]{1,0:T(8,128)(2,1)} %bitcast.85, ...), custom_call_target="tpu_custom_call" | custom-call | flops 45097156608 | bytes 67108864 | tf_op jit(solution)/shard_map/backward/pallas_call | solution.py:2323
  753.1 1.0 slice.46
  754.8 3.2 fusion.3
  758.0 2.9 copy.81
  760.9 1.5 copy.80
  762.4 1.5 copy.79
  763.9 5.3 convert.11
  769.2 3.3 convert.12
  772.5 3.3 convert.13
  775.8 0.8 slice_reduce_fusion
  776.7 1.2 fusion.4
  777.9 2.7 bitcast_convert_fusion
  780.6 1.8 convert_element_type.68
  782.4 1.3 copy.90
  (66 shorter events, 6.7 us)
Async XLA Ops:
  7.2 3.7 copy-start
  7.2 7.8 copy-start.19
  7.2 8.1 %copy-start.20 = (bf16[256,1408]{1,0:T(8,128)(2,1)S(1)}, bf16[256,1408]{1,0:T(8,128)(2,1)}, u32[]{:S(2)}) copy-start(bf16[256,1408]{1,0:T(8,128)(2,1)} %param.31) | copy-start | bytes 2162692
  7.2 773.3 %reduce-scatter.2.cloned.1.call-start = ((), (), s32[]{:S(2)}) async-start(), calls=%async_computation.1 | async-start | bytes 2359296 | tf_op jit(solution)/shard_map/reduce_scatter | solution.py:2506
  7.3 143.7 %copy-start.10 = (s32[1,512]{1,0:T(1,128)}, s32[1,512]{1,0:T(1,128)S(1)}, u32[]{:S(2)}) copy-start(s32[1,512]{1,0:T(1,128)S(1)} %iota_add_fusion.query_at) | copy-start | bytes 6148
  11.0 140.0 %copy-start.9 = (s32[512]{0:T(512)}, s32[512]{0:T(512)S(1)}, u32[]{:S(2)}) copy-start(s32[512]{0:T(512)S(1)} %select_reduce_fusion) | copy-start | bytes 6148
  13.4 137.6 %copy-start.5 = (f32[512,128]{1,0:T(8,128)}, f32[512,128]{1,0:T(8,128)S(1)}, u32[]{:S(2)}) copy-start(f32[512,128]{1,0:T(8,128)S(1)} %get-tuple-element.145.sin_in) | copy-start | bytes 786436
  13.4 137.6 %copy-start.6 = (f32[512,128]{1,0:T(8,128)}, f32[512,128]{1,0:T(8,128)S(1)}, u32[]{:S(2)}) copy-start(f32[512,128]{1,0:T(8,128)S(1)} %get-tuple-element.146.cos_in) | copy-start | bytes 786436
  149.6 115.2 %copy-start.7 = (f32[2048]{0:T(1024)}, f32[2048]{0:T(1024)S(1)}, u32[]{:S(2)}) copy-start(f32[2048]{0:T(1024)S(1)} %get-tuple-element.135) | copy-start | bytes 24580
  149.6 115.2 %copy-start.8 = (f32[2048]{0:T(1024)}, f32[2048]{0:T(1024)S(1)}, u32[]{:S(2)}) copy-start(f32[2048]{0:T(1024)S(1)} %get-tuple-element.134) | copy-start | bytes 24580
  150.9 113.9 %copy-start.2 = (bf16[128,2048]{1,0:T(8,128)(2,1)}, bf16[128,2048]{1,0:T(8,128)(2,1)S(1)}, u32[]{:S(2)}) copy-start(bf16[128,2048]{1,0:T(8,128)(2,1)S(1)} %get-tuple-element.147.tokens_in.own_rows_in) | copy-start | bytes 1572868
  264.9 0.8 copy-start.3
  265.7 0.8 copy-start.11
  266.5 0.6 copy-start.12
  540.3 1.0 copy-start.4
  540.3 1.0 copy-start.21
  763.9 5.3 copy-start.14
  769.2 3.3 copy-start.13
  772.5 3.3 copy-start.16
  772.5 4.2 copy-start.18
  775.8 2.0 copy-start.15
  777.9 4.5 copy-start.17
  782.4 1.3 copy-start.1
Sparse Core Ops, SparseCore 0:
  540.4 94.8 reduce-scatter.1

commit v3 on v1

--- a/solution.py
+++ b/solution.py
@@ -1161,7 +1161,11 @@
 
 
 def weights_kernel(
-    own_in,
+    q_in,
+    k_in,
+    v_in,
+    o_in,
+    side_in,
     pieces_in,
     all_out,
     pieces_out,
@@ -1175,17 +1179,14 @@
 ):
     at = Place()
     depth = at.depth
-    half = own_in.shape[0] // 2
+    half = q_in.shape[0] // 2
     last = depth - 1
 
     def block(k, y, h):
         return all_out.at[at.z + k, y, pl.ds(h * half, half)]
 
     def z_copy(k, h, direction):
-        if k == 0:
-            src = own_in.at[pl.ds(h * half, half)]
-        else:
-            src = block(k, at.y, h)
+        src = block(k, at.y, h)
         slot = last + k - direction
         return remote(
             src,
@@ -1203,19 +1204,25 @@
         )
 
     def y_copy(k, h):
-        src = own_in.at[pl.ds(h * half, half)] if k == 0 else block(k, at.y, h)
+        src = block(k, at.y, h)
         return remote(
-            src, block(k, at.y, h), y_send.at[last + k, h], y_recv.at[last + k, h], at.next_y
+            src, src, y_send.at[last + k, h], y_recv.at[last + k, h], at.next_y
         )
 
-    own_copies = [
-        pltpu.make_async_copy(own_in, all_out.at[at.z, at.y], own_sem.at[0]),
-        pltpu.make_async_copy(pieces_in.at[at.ep], pieces_out.at[at.ep], own_sem.at[1]),
-    ]
-    for copy in own_copies:
+    own_copies, first = [], 0
+    for i, array in enumerate((q_in, k_in, v_in, o_in, side_in)):
+        here = all_out.at[at.z, at.y, :, pl.ds(first, array.shape[1])]
+        own_copies.append(pltpu.make_async_copy(array, here, own_sem.at[i]))
+        first += array.shape[1]
+    piece_copy = pltpu.make_async_copy(
+        pieces_in.at[at.ep], pieces_out.at[at.ep], own_sem.at[len(own_copies)]
+    )
+    for copy in own_copies + [piece_copy]:
         copy.start()
     has_up, has_down = at.z + 1 < depth, at.z > 0
     at.greet_ep()
+    for copy in own_copies:
+        copy.wait()
 
     for h in (0, 1):
         pl.when(has_up)(lambda: z_copy(0, h, 1).start())
@@ -1244,8 +1251,7 @@
                 def _():
                     y_copy(sign * k, h).start()
 
-    for copy in own_copies:
-        copy.wait()
+    piece_copy.wait()
     for copy in swap_copies(*swap, False):
         copy.wait_recv()
     for copy in swap_copies(*swap, True):
@@ -1272,21 +1278,21 @@
                     z_copy(k, h, -sign).wait_send()
 
 
-def gather_over_ep(block, pieces):
-    rows, columns = block.shape
+def gather_over_ep(blocks, pieces):
+    rows, columns = blocks[0].shape[0], sum(block.shape[1] for block in blocks)
     depth = lax.axis_size("ep") // 2
     anywhere = pl.BlockSpec(memory_space=pl.ANY)
     slots = 2 * depth - 1
     out, pieces = pl.pallas_call(
         weights_kernel,
         out_shape=(
-            jax.ShapeDtypeStruct((depth, 2, rows, columns), block.dtype),
+            jax.ShapeDtypeStruct((depth, 2, rows, columns), pieces.dtype),
             jax.ShapeDtypeStruct(pieces.shape, pieces.dtype),
         ),
-        in_specs=[anywhere] * 2,
+        in_specs=[anywhere] * (len(blocks) + 1),
         out_specs=(anywhere,) * 2,
         scratch_shapes=[
-            pltpu.SemaphoreType.DMA((2,)),
+            pltpu.SemaphoreType.DMA((len(blocks) + 1,)),
             pltpu.SemaphoreType.DMA((slots, 2, 2)),
             pltpu.SemaphoreType.DMA((slots, 2)),
             pltpu.SemaphoreType.DMA((slots, 2)),
@@ -1299,7 +1305,7 @@
             flops=0, bytes_accessed=8 * depth * rows * columns, transcendentals=0
         ),
         name="gather_weights",
-    )(block, pieces)
+    )(*blocks, pieces)
     return out.reshape(2 * depth * rows, columns), pieces
 
 
@@ -2409,7 +2415,7 @@
     )
     side_columns = jnp.pad(side_columns, ((0, 0), (0, -side_columns.shape[1] % 128)))
     joined_weights, pieces = gather_over_ep(
-        jnp.concatenate([w_query, w_key, w_value, w_out, side_columns], axis=1),
+        (w_query, w_key, w_value, w_out, side_columns),
         shared_pieces((shared_gate, shared_up, shared_down), ep_count),
     )
     heads_width = w_query.shape[1]

time: 797 us -> 826 us (1.036)
  Pallas kernels: 714 us -> 748 us
    pallas_call x1, Pallas kernels: 123 us -> 155 us  [gather_over_ep(): pl.pallas_call(weights_kernel, out_shape=(jax.ShapeDtypeStruct((depth, 2,...]
    unnamed x53 -> x49, local copies, waits for them, and re-layouts: 17.9 us -> 11.2 us
  transfers between devices with their start and end apart: 1 -> 1, of which waited for: 0 -> 0; matrix products, arithmetic and copies ran while one was open for 4% -> 4% of each run, Pallas kernels for 26% -> 25%
where the time goes in v3:
time: 826 us; the launch traced here: 816 us
  Pallas kernels  748 us (91%)
  local copies, waits for them, and re-layouts  23.7 us (3%)
  other arithmetic  23.5 us (3%)
  between operations  14.8 us (2%)
    pallas_call x1, Pallas kernels, ffn_over_all(): pl.pallas_call(functools.partial(ffn_kernel, units, expert_count), out_sh...  272 us
    pallas_call x1, Pallas kernels, backward(): pl.pallas_call(functools.partial(back_kernel, units, scale), out_shape=(j...  206 us
    pallas_call x1, Pallas kernels, gather_over_ep(): pl.pallas_call(weights_kernel, out_shape=(jax.ShapeDtypeStruct((depth, 2,...  155 us
    pallas_call x1, Pallas kernels, attention_front(): pl.pallas_call(functools.partial(front_kernel, scale), out_shape=(shape((...  115 us
  transfers between devices with their start and end apart: 1, of which 0 were waited for; matrix products, arithmetic and copies ran while one was open for 4% of the time, Pallas kernels for 25%

profile of v3, /device:TPU:13, one launch (start us, length us, event | category | flops | bytes accessed | tf_op | source)
XLA Modules:
  0.0 816.2 jit_solution(14328421204992604002)
XLA Ops:
  7.3 0.9 reduce-window.9
  8.9 0.7 broadcast_in_dim.24
  9.6 0.7 broadcast_in_dim.25
  11.3 0.7 pad_maximum_fusion.3
  12.3 1.1 fusion
  13.4 1.6 copy.71
  16.2 1.5 pad_maximum_fusion.pieces_in
  17.7 155.4 %gather_weights.1 = (bf16[4,2,256,2176]{3,2,1,0:T(8,128)(2,1)}, bf16[8,528,256]{2,1,0:T(8,128)(2,1)}) custom-call(bf16[256,512]{1,0:T(8,128)(2,1)} %q_in.1, bf16[256,512]{1,0:T(8,128)(2,1)} %k_in.1, bf16[256,512]{1,0:T(8,128)(2,1)} %v_in.1, bf16[256,512]{1,0:T(8,128)(2,1)} %o_in.1, bf16[256,128]{1,0:T(8,128)(2,1)} %pad.11.side_in, ...), custom_call_target="tpu_custom_call" | custom-call | bytes 17825792 | tf_op jit(solution)/shard_map/gather_weights/pallas_call | solution.py:1286
  173.1 1.8 convert_reduce_fusion
  174.9 1.3 constant_dynamic-slice_fusion
  176.3 114.7 %attention_front.1 = (bf16[4,2,2,2,128,2176]{5,4,3,2,1,0:T(8,128)(2,1)}, bf16[2048,512]{1,0:T(8,128)(2,1)}, bf16[4,1536,128]{2,1,0:T(8,128)(2,1)}, bf16[4,1536,1...) custom-call(bf16[512,2048]{1,0:T(8,128)(2,1)} %block_in.1, ...), custom_call_target="tpu_custom_call" | custom-call | flops 4294967296 | bytes 17825792 | tf_op jit(solution)/shard_map/attention_front/pallas_call | solution.py:1661
  291.1 0.8 copy-done.3
  291.9 0.8 copy-done.11
  293.3 272.2 %ffn_all_tokens.1 = (bf16[4,2,2,2,128,2048]{5,4,3,2,1,0:T(8,128)(2,1)}, bf16[4,2,512,896]{3,2,1,0:T(8,128)(2,1)}, bf16[4,2,512,1792]{3,2,1,0:T(8,128)(2,1)}, bf1...) custom-call(bf16[128,2048]{1,0:T(8,128)(2,1)} %copy-done.3, ...), custom_call_target="tpu_custom_call" | custom-call | flops 90194313216 | bytes 83886080 | tf_op jit(solution)/shard_map/ffn_all_tokens/pallas_call | solution.py:1060
  565.5 4.2 convolution_convert_fusion
  569.8 1.0 copy-done.4
  570.7 1.6 convolution_select_fusion.side_in
  572.4 206.0 %backward.1 = (f32[256,1536]{1,0:T(8,128)}, f32[256,128]{1,0:T(8,128)}, bf16[2,2,128,2048]{3,2,1,0:T(8,128)(2,1)}, bf16[2,2,128,2048]{3,2,1,0:T(8,128)(2,1)}, bf...) custom-call(bf16[512,2048]{1,0:T(8,128)(2,1)} %bitcast.85, ...), custom_call_target="tpu_custom_call" | custom-call | flops 45097156608 | bytes 67108864 | tf_op jit(solution)/shard_map/backward/pallas_call | solution.py:2295
  778.4 1.0 slice.46
  779.4 0.7 copy.78
  780.1 3.2 fusion.3
  783.2 2.9 copy.81
  786.1 1.5 copy.80
  787.7 1.5 copy.79
  789.2 5.3 convert.11
  794.5 3.3 convert.12
  797.8 3.3 convert.13
  801.1 0.8 slice_reduce_fusion
  802.0 1.2 fusion.4
  803.1 2.7 bitcast_convert_fusion
  805.8 1.8 convert_element_type.68
  807.6 1.3 copy.86
  (62 shorter events, 4.0 us)
Async XLA Ops:
  7.2 3.7 copy-start
  7.2 7.8 copy-start.19
  7.2 8.1 copy-start.20
  7.2 798.6 %reduce-scatter.2.cloned.1.call-start = ((), (), s32[]{:S(2)}) async-start(), calls=%async_computation.1 | async-start | bytes 2359296 | tf_op jit(solution)/shard_map/reduce_scatter | solution.py:2478
  7.3 169.0 %copy-start.10 = (s32[1,512]{1,0:T(1,128)}, s32[1,512]{1,0:T(1,128)S(1)}, u32[]{:S(2)}) copy-start(s32[1,512]{1,0:T(1,128)S(1)} %iota_add_fusion.query_at) | copy-start | bytes 6148
  11.0 165.3 %copy-start.9 = (s32[512]{0:T(512)}, s32[512]{0:T(512)S(1)}, u32[]{:S(2)}) copy-start(s32[512]{0:T(512)S(1)} %select_reduce_fusion) | copy-start | bytes 6148
  13.4 162.9 %copy-start.5 = (f32[512,128]{1,0:T(8,128)}, f32[512,128]{1,0:T(8,128)S(1)}, u32[]{:S(2)}) copy-start(f32[512,128]{1,0:T(8,128)S(1)} %get-tuple-element.145.sin_in) | copy-start | bytes 786436
  13.4 162.9 %copy-start.6 = (f32[512,128]{1,0:T(8,128)}, f32[512,128]{1,0:T(8,128)S(1)}, u32[]{:S(2)}) copy-start(f32[512,128]{1,0:T(8,128)S(1)} %get-tuple-element.146.cos_in) | copy-start | bytes 786436
  174.9 116.2 %copy-start.7 = (f32[2048]{0:T(1024)}, f32[2048]{0:T(1024)S(1)}, u32[]{:S(2)}) copy-start(f32[2048]{0:T(1024)S(1)} %get-tuple-element.135) | copy-start | bytes 24580
  174.9 116.2 %copy-start.8 = (f32[2048]{0:T(1024)}, f32[2048]{0:T(1024)S(1)}, u32[]{:S(2)}) copy-start(f32[2048]{0:T(1024)S(1)} %get-tuple-element.134) | copy-start | bytes 24580
  176.2 114.9 %copy-start.2 = (bf16[128,2048]{1,0:T(8,128)(2,1)}, bf16[128,2048]{1,0:T(8,128)(2,1)S(1)}, u32[]{:S(2)}) copy-start(bf16[128,2048]{1,0:T(8,128)(2,1)S(1)} %get-tuple-element.147.tokens_in.own_rows_in) | copy-start | bytes 1572868
  291.1 0.8 copy-start.3
  291.9 0.8 copy-start.11
  292.7 0.6 copy-start.12
  565.4 4.3 copy-start.21
  569.7 1.0 copy-start.4
  789.2 5.3 copy-start.14
  794.5 3.3 copy-start.13
  797.8 3.3 copy-start.16
  797.8 4.2 copy-start.18
  801.1 2.0 copy-start.15
  803.1 4.5 copy-start.17
  805.8 3.1 copy-start.1
Sparse Core Ops, SparseCore 0:
  569.8 100.7 reduce-scatter.1
